TPU v7x, 128 devices: a whole 4x4x4 slice. The times are simulated.
128 devices in a mesh: grid: 2 (over z_hi), gx: 8 (over z_lo, x), gy: 8 (over y, core).
Axes of the slice: x: 4, y: 4, z: 4 (z_hi: 2, z_lo: 2; z = z_hi * 2 + z_lo), core: 2. Of those that a mesh axis runs over, the one named last changes fastest.
Arguments:
- fields: float32 [2, 9, 48, 192, 384], P('grid', None, 'gx', 'gy'), may hold values from -6 to 6
- material: int32 [2, 48, 192, 384], P('grid', 'gx', 'gy'), may hold values from 0 to 7
- permittivity: float32 [8], replicated, may hold values from 4 to 81
- conductivity: float32 [8], replicated, may hold values from 0.02 to 0.6
- relax_rate: float32 [8], replicated, may hold values from 0.05 to 0.8
- debye_strength: float32 [8], replicated, may hold values from 0.5 to 4
- subgrids: int32 [8, 8, 6], P('gx', 'gy'), may hold values from 0 to 256, as said below
Outputs:
- fields_out: float32 [2, 9, 48, 192, 384], P('grid', None, 'gx', 'gy')
Inputs may be any that keep to these rules, and one draw needn't show every extreme that they name: subgrids[a, b] = (x0, y0, z0, lx, ly, lz): x0 <= 4, y0 <= 16, z0 <= 256; lx is at least 1 and at most 2, ly at least 4 and at most 8, lz at least 64 and at most 128; some block reaches every upper bound.
All inputs are finite; a program needn't handle non-finite values.
Results may differ from a plain program's by a relative error of at most 0.0003.
Values sent between devices are 32-bit elements; how exact they have to be, the bound alone decides.
A program may use at most 128 MiB of HBM per device.

v0:
```python
import jax
import jax.numpy as jnp
from jax import lax
from jax.sharding import PartitionSpec as P

COARSE_STEPS = 3


courant = 0.5
one_third = 1.0 / 3.0


def shifted(value, axis, by):
    peers = lax.axis_size(axis)
    pairs = [(i, i + by) for i in range(peers) if 0 <= i + by < peers]
    return lax.ppermute(value, axis, pairs)


def lookup(material, entries):
    picked = jnp.zeros(material.shape, entries.dtype)
    for candidate in range(entries.shape[0]):
        picked = jnp.where(material == candidate, entries[candidate], picked)
    return picked


def material_factors(material, permittivity, conductivity, relax_rate, debye_strength, factor):
    permit = lookup(material, permittivity)
    damping = lookup(material, conductivity) * factor / (2.0 * permit)
    relaxing = lookup(material, relax_rate) * factor
    return jnp.stack(
        [
            (1.0 - damping) / (1.0 + damping),
            1.0 / (permit * (1.0 + damping)),
            relaxing,
            jnp.exp(-relaxing),
            lookup(material, debye_strength),
        ]
    )


def diff_ahead(values, direction):
    base_cut = [slice(0, -1)] * 3
    moved_cut = [slice(0, -1)] * 3
    moved_cut[direction] = slice(1, None)
    return values[tuple(moved_cut)] - values[tuple(base_cut)]


def diff_behind(values, direction):
    base_cut = [slice(1, None)] * 3
    moved_cut = [slice(1, None)] * 3
    moved_cut[direction] = slice(0, -1)
    return values[tuple(base_cut)] - values[tuple(moved_cut)]


def curl_ahead(padded):
    return jnp.stack(
        [
            diff_ahead(padded[2], 1) - diff_ahead(padded[1], 2),
            diff_ahead(padded[0], 2) - diff_ahead(padded[2], 0),
            diff_ahead(padded[1], 0) - diff_ahead(padded[0], 1),
        ]
    )


def curl_behind(padded):
    return jnp.stack(
        [
            diff_behind(padded[2], 1) - diff_behind(padded[1], 2),
            diff_behind(padded[0], 2) - diff_behind(padded[2], 0),
            diff_behind(padded[1], 0) - diff_behind(padded[0], 1),
        ]
    )


def electric(efield, polarization, rotation, factors):
    return factors[0] * efield + factors[1] * (
        courant * rotation - factors[2] * (factors[4] * efield - polarization)
    )


def relaxation(polarization, efield, factors):
    return factors[3] * polarization + (1.0 - factors[3]) * factors[4] * efield


def fine_update(fields, factors, inside, border, driven):
    efield, hfield, polarization = (fields[0:3], fields[3:6], fields[6:9])
    hfield = inside * (
        hfield - courant * curl_ahead(jnp.pad(efield, ((0, 0), (0, 1), (0, 1), (0, 1))))
    )
    rotation = curl_behind(jnp.pad(hfield, ((0, 0), (1, 0), (1, 0), (1, 0))))
    efield = jnp.where(border, driven, inside * electric(efield, polarization, rotation, factors))
    polarization = inside * relaxation(polarization, efield, factors)
    return jnp.concatenate([efield, hfield, polarization])


def subgrid_masks(extent, cell_shape):
    along_x = lax.broadcasted_iota(jnp.int32, cell_shape, 0)
    along_y = lax.broadcasted_iota(jnp.int32, cell_shape, 1)
    along_z = lax.broadcasted_iota(jnp.int32, cell_shape, 2)
    xlength = 3 * extent[3]
    ylength = 3 * extent[4]
    zlength = 3 * extent[5]
    covered = (along_x < xlength) & (along_y < ylength) & (along_z < zlength)
    xfaces = (along_x == 0) | (along_x == xlength - 1)
    yfaces = (along_y == 0) | (along_y == ylength - 1)
    zfaces = (along_z == 0) | (along_z == zlength - 1)
    border = jnp.stack(
        [covered & (yfaces | zfaces), covered & (xfaces | zfaces), covered & (xfaces | yfaces)]
    )
    return (covered.astype(jnp.float32), border)


def cut_region(efield, extent):
    region_shape = (3, efield.shape[1] // 3, efield.shape[2] // 3, efield.shape[3] // 3)
    return lax.dynamic_slice(efield, (jnp.int32(0), extent[0], extent[1], extent[2]), region_shape)


def upsample(region):
    sizes = region.shape
    spread = jnp.broadcast_to(
        region[:, :, None, :, None, :, None], (sizes[0], sizes[1], 3, sizes[2], 3, sizes[3], 3)
    )
    return spread.reshape(sizes[0], 3 * sizes[1], 3 * sizes[2], 3 * sizes[3])


def restrict(efield):
    sizes = efield.shape
    grouped = efield.reshape(sizes[0], sizes[1] // 3, 3, sizes[2] // 3, 3, sizes[3] // 3, 3)
    return grouped.mean(axis=(2, 4, 6))


def overwrite(fields, restricted, extent):
    region = cut_region(fields[0:3], extent)
    along_x = lax.broadcasted_iota(jnp.int32, region.shape, 1)
    along_y = lax.broadcasted_iota(jnp.int32, region.shape, 2)
    along_z = lax.broadcasted_iota(jnp.int32, region.shape, 3)
    covered = (along_x < extent[3]) & (along_y < extent[4]) & (along_z < extent[5])
    updated = jnp.where(covered, restricted, region)
    return lax.dynamic_update_slice(
        fields, updated, (jnp.int32(0), extent[0], extent[1], extent[2])
    )


def ahead_extend(values, next_x, next_y):
    upper_rows = jnp.concatenate([values, next_x], axis=1)
    corner = jnp.zeros((values.shape[0], 1, 1, values.shape[3]), values.dtype)
    side_rows = jnp.concatenate([next_y, corner], axis=1)
    return jnp.pad(
        jnp.concatenate([upper_rows, side_rows], axis=2), ((0, 0), (0, 0), (0, 0), (0, 1))
    )


def behind_extend(values, prev_x, prev_y):
    upper_rows = jnp.concatenate([prev_x, values], axis=1)
    corner = jnp.zeros((values.shape[0], 1, 1, values.shape[3]), values.dtype)
    side_rows = jnp.concatenate([corner, prev_y], axis=1)
    return jnp.pad(
        jnp.concatenate([side_rows, upper_rows], axis=2), ((0, 0), (0, 0), (0, 0), (1, 0))
    )


def coarse_step(local, factors, coarse):
    efield, hfield, polarization = (local[0:3], local[3:6], local[6:9])
    ahead_x = shifted(efield[:, 0:1], "gx", -1)
    ahead_y = shifted(efield[:, :, 0:1], "gy", -1)
    hfield = lax.cond(
        coarse,
        lambda: hfield - courant * curl_ahead(ahead_extend(efield, ahead_x, ahead_y)),
        lambda: hfield,
    )
    behind_x = shifted(hfield[:, -1:], "gx", 1)
    behind_y = shifted(hfield[:, :, -1:], "gy", 1)
    rotation = lax.cond(
        coarse,
        lambda: curl_behind(behind_extend(hfield, behind_x, behind_y)),
        lambda: jnp.zeros_like(hfield),
    )

    def advance():
        updated = electric(efield, polarization, rotation, factors)
        return (updated, relaxation(polarization, updated, factors))

    efield, polarization = lax.cond(coarse, advance, lambda: (efield, polarization))
    return jnp.concatenate([efield, hfield, polarization])


def body(fields, material, permittivity, conductivity, relax_rate, debye_strength, subgrids):
    coarse = lax.axis_index("grid") == 0
    local = fields[0]
    factor = jnp.where(coarse, 1.0, one_third).astype(local.dtype)
    factors = material_factors(
        material[0], permittivity, conductivity, relax_rate, debye_strength, factor
    )
    extent = subgrids[0, 0]
    inside, border = subgrid_masks(extent, local.shape[1:])
    local = lax.cond(coarse, lambda: local, lambda: local * inside)
    for number in range(COARSE_STEPS):
        earlier = cut_region(local[0:3], extent)
        local = coarse_step(local, factors, coarse)
        latest = cut_region(local[0:3], extent)
        incoming = shifted(jnp.stack([earlier, latest]), "grid", 1)
        for substep in range(1, 4):
            weight = substep / 3.0
            local = lax.cond(
                coarse,
                lambda: local,
                lambda: fine_update(
                    local,
                    factors,
                    inside,
                    border,
                    upsample(incoming[0] + weight * (incoming[1] - incoming[0])),
                ),
            )
        restricted = lax.cond(coarse, lambda: jnp.zeros_like(earlier), lambda: restrict(local[0:3]))
        received = shifted(restricted, "grid", -1)
        local = lax.cond(coarse, lambda: overwrite(local, received, extent), lambda: local)
    return local[None]


def solution(mesh):
    in_specs = (
        P("grid", None, "gx", "gy", None),
        P("grid", "gx", "gy", None),
        P(),
        P(),
        P(),
        P(),
        P("gx", "gy", None),
    )
    out_specs = P("grid", None, "gx", "gy", None)
    return jax.shard_map(body, mesh=mesh, in_specs=in_specs, out_specs=out_specs, check_vma=False)
```

profile of v0, /device:TPU:40, one launch (start us, length us, event | category | flops | bytes accessed | tf_op | source)
XLA Modules:
  0.0 659.1 jit_solution(4351503221420194762)
XLA Ops:
  0.0 1.5 fusion.310
  3.6 1.6 conditional.25
  3.6 1.6 copy.14
  5.8 4.2 collective-permute-start
  10.7 2.1 collective-permute-start.1
  12.8 2.5 fusion.309
  17.3 5.4 exponential_bitcast_fusion
  22.7 10.2 %subtract_divide_fusion = f32[1,6,24,384]{3,2,1,0:T(8,128)S(1)} fusion(pred[1,6,24,384]{3,2,1,0:T(8,128)(4,1)S(1)} %get-tuple-element.651, pred[1,6,24,384]{3,2,1,0:T(8,128)(4,1)S(1)} %get-tuple-element.650, pred[1,6,24,384]{3,2,1,0:T(8,128)(4,1)S(1)} %get-tuple-element.649, pred[1,6,24,384]{3,2,1,0:T(8,128)(4,1)S(1)} %get-tuple-element.648, ...), kind=kLoop, calls=%fused_computation.615 | loop fusion | flops 1216512 | bytes 663620 | tf_op jit(solution)/shard_map/div | solution.py:32
  32.9 10.2 %multiply_divide_fusion = f32[1,6,24,384]{3,2,1,0:T(8,128)S(1)} fusion(pred[1,6,24,384]{3,2,1,0:T(8,128)(4,1)S(1)} %get-tuple-element.651, pred[1,6,24,384]{3,2,1,0:T(8,128)(4,1)S(1)} %get-tuple-element.650, pred[1,6,24,384]{3,2,1,0:T(8,128)(4,1)S(1)} %get-tuple-element.649, pred[1,6,24,384]{3,2,1,0:T(8,128)(4,1)S(1)} %get-tuple-element.648, ...), kind=kLoop, calls=%fused_computation.614 | loop fusion | flops 1216512 | bytes 663620 | tf_op jit(solution)/shard_map/div | solution.py:33
  43.9 5.3 select_select_fusion
  55.4 3.4 conditional.26
  56.7 2.0 fusion
  60.6 2.4 collective-permute-start.2
  63.0 1.9 collective-permute-start.3
  65.8 6.9 %collective-permute-done.3 = f32[3,1,24,384]{3,2,1,0:T(8,128)S(1)} collective-permute-done((f32[3,1,24,384]{3,2,1,0:T(8,128)S(1)}, f32[3,1,24,384]{3,2,1,0:T(8,128)S(1)}, u32[]{:S(2)}, u32[]{:S(2)}) %collective-permute-start.3) | collective-permute-done | bytes 110624 | tf_op jit(solution)/shard_map/ppermute | solution.py:16
  72.7 2.2 conditional.27
  76.6 1.9 collective-permute-start.4
  78.5 1.6 pad_maximum_fusion.12
  80.4 8.7 %conditional.32 = (f32[3,2,8,128]{3,2,1,0:T(8,128)}) conditional(s32[]{:T(128)} %convert_element_type.32, f32[9,6,24,384]{3,2,1,0:T(8,128)S(1)} %get-tuple-element.895, () %tuple.169), branch_computations={%region_14.16_spmd, %region_16.17_spmd} | conditional | flops 165888 | bytes 3391500 | solution.py:215
  90.4 150.0 %collective-permute-done.5 = f32[3,2,8,128]{3,2,1,0:T(8,128)} collective-permute-done((f32[3,2,8,128]{3,2,1,0:T(8,128)}, f32[3,2,8,128]{3,2,1,0:T(8,128)}, u32[]{:S(2)}, u32[]{:S(2)}) %collective-permute-start.5) | collective-permute-done | bytes 24608 | tf_op jit(solution)/shard_map/ppermute | solution.py:16
  240.4 13.1 %conditional.33 = (f32[9,6,24,384]{3,2,1,0:T(8,128)S(1)}) conditional(s32[]{:T(128)} %convert_element_type.32, f32[9,6,24,384]{3,2,1,0:T(8,128)S(1)} %get-tuple-element.895, (s32[6]{0:T(128)S(1)}, f32[9,6,24,384]{3,2,1,0:T(8,128)S(1)}, f32[3,2,8,128]{3,2,1,0:T(8,128)}) %tuple.455), branch_computations={%region_17.18_spmd, %region_18.19_spmd} | conditional | flops 18579 | bytes 1450446 | solution.py:217
  250.6 2.9 dynamic_update_slice.7
  253.6 1.9 collective-permute-start.6
  255.5 1.9 collective-permute-start.7
  260.2 3.2 conditional.34
  265.4 2.7 collective-permute-start.8
  268.0 3.9 collective-permute-start.9
  273.5 4.2 collective-permute-done.9
  278.3 2.3 conditional.35
  282.3 1.9 collective-permute-start.10
  284.2 1.6 pad_maximum_fusion.13
  286.1 8.5 %conditional.40 = (f32[3,2,8,128]{3,2,1,0:T(8,128)}) conditional(s32[]{:T(128)} %convert_element_type.32, f32[9,6,24,384]{3,2,1,0:T(8,128)S(1)} %get-tuple-element.903, () %tuple.179), branch_computations={%region_31.33_spmd, %region_33.34_spmd} | conditional | flops 165888 | bytes 3391500 | solution.py:215
  295.9 149.6 %collective-permute-done.11 = f32[3,2,8,128]{3,2,1,0:T(8,128)} collective-permute-done((f32[3,2,8,128]{3,2,1,0:T(8,128)}, f32[3,2,8,128]{3,2,1,0:T(8,128)}, u32[]{:S(2)}, u32[]{:S(2)}) %collective-permute-start.11) | collective-permute-done | bytes 24608 | tf_op jit(solution)/shard_map/ppermute | solution.py:16
  445.5 13.1 %conditional.41 = (f32[9,6,24,384]{3,2,1,0:T(8,128)S(1)}) conditional(s32[]{:T(128)} %convert_element_type.32, f32[9,6,24,384]{3,2,1,0:T(8,128)S(1)} %get-tuple-element.903, (s32[6]{0:T(128)S(1)}, f32[9,6,24,384]{3,2,1,0:T(8,128)S(1)}, f32[3,2,8,128]{3,2,1,0:T(8,128)}) %tuple.456), branch_computations={%region_34.35_spmd, %region_35.36_spmd} | conditional | flops 18579 | bytes 1450446 | solution.py:217
  455.7 2.9 dynamic_update_slice.8
  458.7 1.9 collective-permute-start.12
  460.6 1.9 collective-permute-start.13
  465.3 3.2 conditional.42
  470.5 2.4 collective-permute-start.14
  472.9 3.9 collective-permute-start.15
  478.3 4.3 collective-permute-done.15
  483.3 2.3 conditional.43
  487.2 1.9 collective-permute-start.16
  489.1 1.6 pad_maximum_fusion.14
  491.1 2.8 conditional.48
  495.2 151.8 %collective-permute-done.17 = f32[3,2,8,128]{3,2,1,0:T(8,128)S(1)} collective-permute-done((f32[3,2,8,128]{3,2,1,0:T(8,128)S(1)}, f32[3,2,8,128]{3,2,1,0:T(8,128)S(1)}, u32[]{:S(2)}, u32[]{:S(2)}) %collective-permute-start.17) | collective-permute-done | bytes 24608 | tf_op jit(solution)/shard_map/ppermute | solution.py:16
  647.0 10.2 %conditional.49 = (f32[1,9,6,24,384]{4,3,2,1,0:T(8,128)S(1)}) conditional(s32[]{:T(128)} %convert_element_type.32, f32[9,6,24,384]{3,2,1,0:T(8,128)S(1)} %get-tuple-element.911, (f32[9,6,24,384]{3,2,1,0:T(8,128)S(1)}, s32[6]{0:T(128)S(1)}, f32[3,2,8,128]{3,2,1,0:T(8,128)S(1)}) %tuple.457), branch_computations={%region_51.52_spmd, %region_52.53_spmd} | conditional | flops 18579 | bytes 1450446 | solution.py:217
  655.2 2.1 dynamic_update_slice.9
  (162 shorter events, 62.6 us)
Async XLA Ops:
  5.2 5.5 copy-start.32
  5.8 49.5 %collective-permute-start = (f32[3,1,24,384]{3,2,1,0:T(8,128)}, f32[3,1,24,384]{3,2,1,0:T(8,128)}, u32[]{:S(2)}, u32[]{:S(2)}) collective-permute-start(f32[3,1,24,384]{3,2,1,0:T(8,128)} %slice.1700), channel_id=1, source_target_pairs={{8,0},{16,8},{24,16},{32,24},{40,32},{48,40},{56,48},{9,1},{17,9},... | collective-permute-start | bytes 331784 | tf_op jit(solution)/shard_map/ppermute | solution.py:16
  10.7 4.5 copy-start.55
  10.7 5.2 copy-start.56
  10.7 5.9 copy-start.57
  10.7 6.6 copy-start.52
  10.7 44.6 %collective-permute-start.1 = (f32[3,6,1,384]{3,2,1,0:T(1,128)}, f32[3,6,1,384]{3,2,1,0:T(1,128)}, u32[]{:S(2)}, u32[]{:S(2)}) collective-permute-start(f32[3,6,1,384]{3,2,1,0:T(1,128)} %slice.1701), channel_id=1, source_target_pairs={{1,0},{2,1},{3,2},{4,3},{5,4},{6,5},{7,6},{9,8},{10,9},{11,10},{12... | collective-permute-start | bytes 82952 | tf_op jit(solution)/shard_map/ppermute | solution.py:16
  15.2 27.8 %copy-start.58 = (f32[8]{0:T(128)S(1)}, f32[8]{0:T(128)}, u32[]{:S(2)}) copy-start(f32[8]{0:T(128)} %param.62) | copy-start | bytes 100
  60.6 5.2 collective-permute-start.2
  63.0 9.7 %collective-permute-start.3 = (f32[3,1,24,384]{3,2,1,0:T(8,128)S(1)}, f32[3,1,24,384]{3,2,1,0:T(8,128)S(1)}, u32[]{:S(2)}, u32[]{:S(2)}) collective-permute-start(f32[3,1,24,384]{3,2,1,0:T(8,128)S(1)} %slice.1703), channel_id=1, source_target_pairs={{0,8},{8,16},{16,24},{24,32},{32,40},{40,48},{48,56},{1,9},{9,17},... | collective-permute-start | bytes 331784 | tf_op jit(solution)/shard_map/ppermute | solution.py:16
  75.7 2.8 copy-start.1
  75.7 2.8 copy-start.24
  76.6 3.5 collective-permute-start.4
  80.4 160.0 %copy-start.51 = (s32[1,1,6]{2,1,0:T(1,128)S(1)}, s32[1,1,6]{2,1,0:T(1,128)}, u32[]{:S(2)}) copy-start(s32[1,1,6]{2,1,0:T(1,128)} %param.63) | copy-start | bytes 76
  89.1 151.3 %collective-permute-start.5 = (f32[3,2,8,128]{3,2,1,0:T(8,128)}, f32[3,2,8,128]{3,2,1,0:T(8,128)}, u32[]{:S(2)}, u32[]{:S(2)}) collective-permute-start(f32[3,2,8,128]{3,2,1,0:T(8,128)} %get-tuple-element.896), channel_id=1, source_target_pairs={{64,0},{65,1},{66,2},{67,3},{68,4},{69,5},{70,6},{71,7},{72,8},{73... | collective-permute-start | bytes 73736 | tf_op jit(solution)/shard_map/ppermute | solution.py:16
  253.6 6.6 %collective-permute-start.6 = (f32[3,1,24,384]{3,2,1,0:T(8,128)S(1)}, f32[3,1,24,384]{3,2,1,0:T(8,128)S(1)}, u32[]{:S(2)}, u32[]{:S(2)}) collective-permute-start(f32[3,1,24,384]{3,2,1,0:T(8,128)S(1)} %slice.1707), channel_id=1, source_target_pairs={{8,0},{16,8},{24,16},{32,24},{40,32},{48,40},{56,48},{9,1},{17,9},... | collective-permute-start | bytes 331784 | tf_op jit(solution)/shard_map/ppermute | solution.py:16
  255.5 3.5 collective-permute-start.7
  261.4 1.1 copy-start.9
  262.6 0.8 copy-start.10
  265.4 8.1 %collective-permute-start.8 = (f32[3,6,1,384]{3,2,1,0:T(1,128)S(1)}, f32[3,6,1,384]{3,2,1,0:T(1,128)S(1)}, u32[]{:S(2)}, u32[]{:S(2)}) collective-permute-start(f32[3,6,1,384]{3,2,1,0:T(1,128)S(1)} %slice.1709), channel_id=1, source_target_pairs={{0,1},{1,2},{2,3},{3,4},{4,5},{5,6},{6,7},{8,9},{9,10},{10,11},{11... | collective-permute-start | bytes 82952 | tf_op jit(solution)/shard_map/ppermute | solution.py:16
  268.0 9.6 %collective-permute-start.9 = (f32[3,1,24,384]{3,2,1,0:T(8,128)S(1)}, f32[3,1,24,384]{3,2,1,0:T(8,128)S(1)}, u32[]{:S(2)}, u32[]{:S(2)}) collective-permute-start(f32[3,1,24,384]{3,2,1,0:T(8,128)S(1)} %slice.1710), channel_id=1, source_target_pairs={{0,8},{8,16},{16,24},{24,32},{32,40},{40,48},{48,56},{1,9},{9,17},... | collective-permute-start | bytes 331784 | tf_op jit(solution)/shard_map/ppermute | solution.py:16
  273.5 4.2 copy-start.59
  277.7 0.6 copy-start.53
  278.3 2.3 copy-start.3
  278.3 2.3 copy-start.26
  281.4 2.8 copy-start.4
  281.4 2.8 copy-start.27
  282.3 3.5 collective-permute-start.10
  294.6 150.9 %collective-permute-start.11 = (f32[3,2,8,128]{3,2,1,0:T(8,128)}, f32[3,2,8,128]{3,2,1,0:T(8,128)}, u32[]{:S(2)}, u32[]{:S(2)}) collective-permute-start(f32[3,2,8,128]{3,2,1,0:T(8,128)} %get-tuple-element.904), channel_id=1, source_target_pairs={{64,0},{65,1},{66,2},{67,3},{68,4},{69,5},{70,6},{71,7},{72,8},{73... | collective-permute-start | bytes 73736 | tf_op jit(solution)/shard_map/ppermute | solution.py:16
  458.7 6.6 %collective-permute-start.12 = (f32[3,1,24,384]{3,2,1,0:T(8,128)S(1)}, f32[3,1,24,384]{3,2,1,0:T(8,128)S(1)}, u32[]{:S(2)}, u32[]{:S(2)}) collective-permute-start(f32[3,1,24,384]{3,2,1,0:T(8,128)S(1)} %slice.1714), channel_id=1, source_target_pairs={{8,0},{16,8},{24,16},{32,24},{40,32},{48,40},{56,48},{9,1},{17,9},... | collective-permute-start | bytes 331784 | tf_op jit(solution)/shard_map/ppermute | solution.py:16
  460.6 3.5 collective-permute-start.13
  466.5 1.1 copy-start.12
  467.7 0.8 copy-start.13
  470.5 7.8 %collective-permute-start.14 = (f32[3,6,1,384]{3,2,1,0:T(1,128)S(1)}, f32[3,6,1,384]{3,2,1,0:T(1,128)S(1)}, u32[]{:S(2)}, u32[]{:S(2)}) collective-permute-start(f32[3,6,1,384]{3,2,1,0:T(1,128)S(1)} %slice.1716), channel_id=1, source_target_pairs={{0,1},{1,2},{2,3},{3,4},{4,5},{5,6},{6,7},{8,9},{9,10},{10,11},{11... | collective-permute-start | bytes 82952 | tf_op jit(solution)/shard_map/ppermute | solution.py:16
  472.9 9.7 %collective-permute-start.15 = (f32[3,1,24,384]{3,2,1,0:T(8,128)S(1)}, f32[3,1,24,384]{3,2,1,0:T(8,128)S(1)}, u32[]{:S(2)}, u32[]{:S(2)}) collective-permute-start(f32[3,1,24,384]{3,2,1,0:T(8,128)S(1)} %slice.1717), channel_id=1, source_target_pairs={{0,8},{8,16},{16,24},{24,32},{32,40},{40,48},{48,56},{1,9},{9,17},... | collective-permute-start | bytes 331784 | tf_op jit(solution)/shard_map/ppermute | solution.py:16
  478.3 4.3 copy-start.60
  482.6 0.6 copy-start.54
  483.3 2.3 copy-start.6
  483.3 2.3 copy-start.29
  486.3 2.8 copy-start.7
  486.3 2.8 copy-start.30
  487.2 3.5 collective-permute-start.16
  493.9 153.1 %collective-permute-start.17 = (f32[3,2,8,128]{3,2,1,0:T(8,128)S(1)}, f32[3,2,8,128]{3,2,1,0:T(8,128)S(1)}, u32[]{:S(2)}, u32[]{:S(2)}) collective-permute-start(f32[3,2,8,128]{3,2,1,0:T(8,128)S(1)} %get-tuple-element.912), channel_id=1, source_target_pairs={{64,0},{65,1},{66,2},{67,3},{68,4},{69,5},{70,6},{71,7},{72,8},{73... | collective-permute-start | bytes 73736 | tf_op jit(solution)/shard_map/ppermute | solution.py:16
  657.3 1.3 copy-start
where the time goes:
time: 672 us; the launch traced here: 659 us
  waiting for transfers between devices  470 us (70%)
  other arithmetic  61.9 us (9%)
  local copies, waits for them, and re-layouts  42.3 us (6%)
  starting transfers between devices  40.7 us (6%)
  loops' own time  35.8 us (5%)
  between operations  8.4 us (1%)
    ppermute x18, waiting for transfers between devices, shifted(): return lax.ppermute(value, axis, pairs)  470 us
    ppermute x18, starting transfers between devices, shifted(): return lax.ppermute(value, axis, pairs)  40.7 us
    another operation x3, loops' own time, body(): lax.cond(coarse, lambda: jnp.zeros_like(earlier), lambda: restrict(local[...  18.8 us
    another operation x3, loops' own time, body(): lax.cond(coarse, lambda: overwrite(local, received, extent), lambda: local)  15.9 us
  transfers between devices with their start and end apart: 18, of which 11 were waited for; matrix products, arithmetic and copies ran while one was open for 7% of the time, Pallas kernels for 0%

commit v1 on v0

v1 whole, which is shorter than its diff:
```python
import functools

import jax
import jax.numpy as jnp
from jax import lax
from jax.experimental import pallas as pl
from jax.experimental.pallas import tpu as pltpu
from jax.sharding import PartitionSpec as P

MESH = pl.DeviceIdType.MESH
STEPS = 3
F32 = jnp.float32

TO_NEXT = ((-1, 0), (0, -1), (1, 0), (0, 1), (1, -1), (-1, 1))
XE, YE, XG, YG, C1, C2 = range(6)


def lane_iota():
    return lax.broadcasted_iota(jnp.int32, (8, 128), 1)


def row_iota():
    return lax.broadcasted_iota(jnp.int32, (8, 128), 0)


def pick(tile, index):
    return jnp.take_along_axis(tile, index, axis=1, mode="promise_in_bounds")


def zfwd(v):
    n = v.shape[-1]
    lanes = lax.broadcasted_iota(jnp.int32, v.shape, v.ndim - 1)
    return jnp.where(lanes == n - 1, 0.0, pltpu.roll(v, n - 1, v.ndim - 1))


def zbwd(v):
    lanes = lax.broadcasted_iota(jnp.int32, v.shape, v.ndim - 1)
    return jnp.where(lanes == 0, 0.0, pltpu.roll(v, 1, v.ndim - 1))


def yfwd(t):
    return jnp.where(row_iota() == 7, 0.0, pltpu.roll(t, 7, 0))


def ybwd(t):
    return jnp.where(row_iota() == 0, 0.0, pltpu.roll(t, 1, 0))


def tables(permit, conduct, relax, debye, factor, courant):
    lane = lane_iota()

    def spread(ref):
        out = jnp.ones((8, 128), F32)
        for m in range(8):
            out = jnp.where(lane == m, ref[m], out)
        return out

    eps = spread(permit)
    damping = spread(conduct) * factor / (2.0 * eps)
    f0 = (1.0 - damping) / (1.0 + damping)
    f1 = 1.0 / (eps * (1.0 + damping))
    f2 = spread(relax) * factor
    f3 = jnp.exp(-f2)
    f4 = spread(debye)
    return f0 - f1 * f2 * f4, courant * f1, f1 * f2, f3, (1.0 - f3) * f4


def kernel(
    nx, ny,
    fields, material, permit, conduct, relax, debye, subgrids, out,
    e, h, p, k, stage, mat, ff, fk, pk, pln, ear, drv,
    xe_s, ye_s, xg_s, yg_s, c1_s, c2_s,
    xe_r, ye_r, xg_r, yg_r, c1_r, c2_r,
    lat_s, lat_r, del_s, del_r,
    lsem, hs, hr, bs, br, ds, dr,
):
    grid = lax.axis_index("grid")
    ga = lax.axis_index("gx")
    gb = lax.axis_index("gy")
    coarse = grid == 0
    x0, y0, z0 = subgrids[0, 0, 0], subgrids[0, 0, 1], subgrids[0, 0, 2]
    lx, ly, lz = subgrids[0, 0, 3], subgrids[0, 0, 4], subgrids[0, 0, 5]
    sends = (xe_s, ye_s, xg_s, yg_s, c1_s, c2_s)
    recvs = (xe_r, ye_r, xg_r, yg_r, c1_r, c2_r)

    def exists(dx, dy):
        return (ga + dx >= 0) & (ga + dx < nx) & (gb + dy >= 0) & (gb + dy < ny)

    partner = (1 - grid, ga, gb)

    def local_copies():
        e_in = pltpu.make_async_copy(fields.at[0, 0:3], e.at[:, 0:6, 0:24, :], lsem.at[0])
        h_in = pltpu.make_async_copy(fields.at[0, 3:6], h.at[:, 1:7, 8:32, :], lsem.at[1])
        p_in = pltpu.make_async_copy(fields.at[0, 6:9], p, lsem.at[2])
        return e_in, h_in, p_in

    m_in = [pltpu.make_async_copy(material.at[0, :, :, pl.ds(128 * v, 128)], mat.at[v], lsem.at[3 + v]) for v in range(3)]
    for cp in m_in:
        cp.start()

    @pl.when(coarse)
    def _():
        for cp in local_copies():
            cp.start()
        for ref in (ye_s, yg_s, pk, pln) + recvs:
            ref[...] = jnp.zeros_like(ref)

    f_in = [pltpu.make_async_copy(fields.at[0, :, :, :, pl.ds(128 * v, 128)], stage.at[v], lsem.at[v]) for v in range(3)]

    @pl.when(jnp.logical_not(coarse))
    def _():
        for cp in f_in:
            cp.start()

    barrier = pltpu.get_barrier_semaphore()
    pl.semaphore_signal(barrier, inc=1, device_id=partner, device_id_type=MESH)
    count = jnp.int32(1)
    for dx, dy in TO_NEXT:
        there = exists(dx, dy) & coarse
        count = count + there.astype(jnp.int32)

        @pl.when(there)
        def _():
            pl.semaphore_signal(barrier, inc=1, device_id=(grid, ga + dx, gb + dy), device_id_type=MESH)

    pl.semaphore_wait(barrier, count)

    def halo_copy(m, n):
        dx, dy = TO_NEXT[m]
        return pltpu.make_async_remote_copy(
            src_ref=sends[m].at[n], dst_ref=recvs[m].at[n], send_sem=hs.at[m, n], recv_sem=hr.at[m, n],
            device_id=(grid, jnp.clip(ga + dx, 0, nx - 1), jnp.clip(gb + dy, 0, ny - 1)), device_id_type=MESH)

    def lat_copy(n):
        return pltpu.make_async_remote_copy(
            src_ref=lat_s.at[n], dst_ref=lat_r.at[n], send_sem=bs.at[n], recv_sem=br.at[n],
            device_id=partner, device_id_type=MESH)

    def del_copy(n):
        return pltpu.make_async_remote_copy(
            src_ref=del_s.at[n], dst_ref=del_r.at[n], send_sem=ds.at[n], recv_sem=dr.at[n],
            device_id=partner, device_id_type=MESH)

    rows, lanes = row_iota(), lane_iota()
    row_ok = [(rows + 8 * u >= y0) & (rows + 8 * u < y0 + 8) for u in range(3)]
    lane_ok = [(lanes + 128 * v >= z0) & (lanes + 128 * v < z0 + 128) for v in range(3)]

    @pl.when(coarse)
    def _():
        e_in, h_in, p_in = local_copies()
        flag_x = jnp.where(ga > 0, 1.0, 0.0).astype(F32)
        flag_y = jnp.where(gb > 0, 1.0, 0.0).astype(F32)

        def cut(n):
            for i in range(2):
                for c in range(3):
                    tile = jnp.zeros((8, 128), F32)
                    for u in range(3):
                        for v in range(3):
                            here = e[c, x0 + i, 8 * u:8 * u + 8, 128 * v:128 * v + 128]
                            tile = jnp.where(row_ok[u] & lane_ok[v], here, tile)
                    lat_s[n, c, i] = tile
            lat_copy(n).start()

        def place(n):
            def at_x(x, carry):
                s0 = jnp.where(x == x0, 1.0, 0.0).astype(F32)
                s1 = jnp.where(x == x0 + 1, 1.0, 0.0).astype(F32)
                for c in range(3):
                    tile = s0 * del_r[n, c, 0] + s1 * del_r[n, c, 1]
                    for u in range(3):
                        for v in range(3):
                            spot = (c, x, slice(8 * u, 8 * u + 8), slice(128 * v, 128 * v + 128))
                            e[spot] = e[spot] + jnp.where(row_ok[u] & lane_ok[v], tile, 0.0)
                return carry

            lax.fori_loop(0, 6, at_x, 0)

        def send_halos(n):
            for x in range(6):
                ye_s[n, 0, x:x + 1, :] = e[0, x, 0:1, :]
                ye_s[n, 1, x:x + 1, :] = e[2, x, 0:1, :]
                for c in range(3):
                    pk[c, x:x + 1, :] = e[c, x, 23:24, :]
                pk[3, x:x + 1, :] = h[0, x + 1, 31:32, :]
                pk[4, x:x + 1, :] = h[2, x + 1, 31:32, :]
            xe_s[n] = e[1:3, 0, 0:24, :]
            ex, ey, ez = e[0, 5, 0:24, :], e[1, 5, 0:24, :], e[2, 5, 0:24, :]
            wide = lax.broadcasted_iota(jnp.int32, (24, 384), 0)
            exy = jnp.where(wide == 23, 0.0, e[0, 5, 1:25, :])
            xg_s[n, 0] = h[1, 6, 8:32, :] - 0.5 * (zfwd(ex) - ex + ez)
            xg_s[n, 1] = h[2, 6, 8:32, :] + 0.5 * (ey + exy - ex)
            px, py, pz = pk[0, 0:8, :], pk[1, 0:8, :], pk[2, 0:8, :]
            yg_s[n, 0] = pk[3, 0:8, :] + 0.5 * (pz + zfwd(py) - py)
            yg_s[n, 1] = pk[4, 0:8, :] - 0.5 * (pk[1, 1:9, :] - py + px)
            c1_s[n] = jnp.broadcast_to(e[0, 5, 0:1, :], (8, 384))
            c2_s[n] = jnp.broadcast_to(e[1, 0, 23:24, :], (8, 384))
            for m, (dx, dy) in enumerate(TO_NEXT):
                @pl.when(exists(dx, dy))
                def _():
                    halo_copy(m, n).start()

        def take_halos(n):
            for m, (dx, dy) in enumerate(TO_NEXT):
                @pl.when(exists(-dx, -dy))
                def _():
                    halo_copy(m, n).wait_recv()
            e[1:3, 6, 0:24, :] = xe_r[n]
            h[1, 0, 8:32, :] = flag_x * (xg_r[n, 0] + 0.5 * e[2, 0, 0:24, :])
            wide = lax.broadcasted_iota(jnp.int32, (24, 384), 0)
            corner = jnp.where(wide == 23, jnp.broadcast_to(c1_r[n, 0:1, :], (24, 384)), 0.0)
            h[2, 0, 8:32, :] = flag_x * (xg_r[n, 1] - 0.5 * (e[1, 0, 0:24, :] - corner))
            plane = lax.broadcasted_iota(jnp.int32, (8, 384), 0)
            pln[0] = flag_y * (yg_r[n, 0] - 0.5 * ye_s[n, 1])
            pln[1] = flag_y * (yg_r[n, 1] + 0.5 * (ye_s[n, 0] - jnp.where(plane == 5, c2_r[n], 0.0)))
            for x in range(6):
                e[0, x, 24:25, :] = ye_r[n, 0, x:x + 1, :]
                e[2, x, 24:25, :] = ye_r[n, 1, x:x + 1, :]
                h[0, x + 1, 7:8, :] = pln[0, x:x + 1, :]
                h[2, x + 1, 7:8, :] = pln[1, x:x + 1, :]

        def update():
            def at_x(x, carry):
                for u in range(3):
                    r = slice(8 * u, 8 * u + 8)
                    ra = slice(8 * u + 1, 8 * u + 9)
                    hr_ = slice(8 * u + 8, 8 * u + 16)
                    hb = slice(8 * u + 7, 8 * u + 15)
                    ex, ey, ez = e[0, x, r, :], e[1, x, r, :], e[2, x, r, :]
                    hx = h[0, x + 1, hr_, :] - 0.5 * ((e[2, x, ra, :] - ez) - (zfwd(ey) - ey))
                    hy = h[1, x + 1, hr_, :] - 0.5 * ((zfwd(ex) - ex) - (e[2, x + 1, r, :] - ez))
                    hz = h[2, x + 1, hr_, :] - 0.5 * ((e[1, x + 1, r, :] - ey) - (e[0, x, ra, :] - ex))
                    h[0, x + 1, hr_, :] = hx
                    h[1, x + 1, hr_, :] = hy
                    h[2, x + 1, hr_, :] = hz
                    cx = (hz - h[2, x + 1, hb, :]) - (hy - zbwd(hy))
                    cy = (hx - zbwd(hx)) - (hz - h[2, x, hr_, :])
                    cz = (hy - h[1, x, hr_, :]) - (hx - h[0, x + 1, hb, :])
                    ka, kc, kb, kf, kg = (k[q, x, r, :] for q in range(5))
                    for c, (old, curl) in enumerate(((ex, cx), (ey, cy), (ez, cz))):
                        pol = p[c, x, r, :]
                        new = ka * old + kc * curl + kb * pol
                        e[c, x, r, :] = new
                        p[c, x, r, :] = kf * pol + kg * new
                return carry

            lax.fori_loop(0, 6, at_x, 0)

        e_in.wait()
        cut(STEPS)
        h_in.wait()
        send_halos(0)
        for cp in m_in:
            cp.wait()
        tabs = tables(permit, conduct, relax, debye, 1.0, 0.5)

        def factors(x, carry):
            for u in range(3):
                for v in range(3):
                    spot = (x, slice(8 * u, 8 * u + 8), slice(128 * v, 128 * v + 128))
                    here = mat[v, x, 8 * u:8 * u + 8, :]
                    for q in range(5):
                        k[(q,) + spot] = pick(tabs[q], here)
            return carry

        lax.fori_loop(0, 6, factors, 0)
        p_in.wait()

        def step(n, carry):
            @pl.when(n > 0)
            def _():
                del_copy(n - 1).wait_recv()
                place(n - 1)
                send_halos(n)

            take_halos(n)
            update()
            cut(n)
            return carry

        lax.fori_loop(0, STEPS, step, 0)
        h_out = pltpu.make_async_copy(h.at[:, 1:7, 8:32, :], out.at[0, 3:6], lsem.at[1])
        p_out = pltpu.make_async_copy(p, out.at[0, 6:9], lsem.at[2])
        h_out.start()
        p_out.start()
        del_copy(STEPS - 1).wait_recv()
        place(STEPS - 1)
        e_out = pltpu.make_async_copy(e.at[:, 0:6, 0:24, :], out.at[0, 0:3], lsem.at[0])
        e_out.start()

        def drain(n, carry):
            for m, (dx, dy) in enumerate(TO_NEXT):
                @pl.when(exists(dx, dy))
                def _():
                    halo_copy(m, n).wait_send()
            return carry

        lax.fori_loop(0, STEPS, drain, 0)
        for n in range(STEPS + 1):
            lat_copy(n).wait_send()
        h_out.wait()
        p_out.wait()
        e_out.wait()

    @pl.when(jnp.logical_not(coarse))
    def _():
        inside = (rows < ly) & (lanes < lz)
        two = lx == 2

        def inside_x(x):
            return jnp.where((x < 3) | two, 1, 0).astype(jnp.int32)

        tabs = tables(permit, conduct, relax, debye, 1.0 / 3.0, 0.25)
        spread = [3 * lanes + r for r in range(3)]
        packed = [(lanes + 128 * v) for v in range(3)]
        third = [q // 3 for q in packed]
        phase = [q - 3 * t for q, t in zip(packed, third)]

        def gather_in(ref, lead, ry):
            parts = [ref[(v,) + lead + (pl.ds(ry, 8, stride=3), slice(None))] for v in range(3)]
            tiles = []
            for r in range(3):
                at, src = spread[r] & 127, spread[r] >> 7
                got = [pick(part, at) for part in parts]
                tiles.append(jnp.where(src == 0, got[0], jnp.where(src == 1, got[1], got[2])))
            return tiles

        for cp in m_in:
            cp.wait()

        def fine_factors(x, carry):
            ok = inside & (inside_x(x) + jnp.zeros((8, 128), jnp.int32) > 0)
            for ry in range(3):
                for r, here in enumerate(gather_in(mat, (x,), ry)):
                    for q in range(5):
                        value = pick(tabs[q], here)
                        if q == 1 or q == 2:
                            value = jnp.where(ok, value, 0.0)
                        fk[q, x, 3 * ry + r] = value
            return carry

        lax.fori_loop(0, 6, fine_factors, 0)
        for cp in f_in:
            cp.wait()
        for c in range(3):
            ff[c, 6] = jnp.zeros((9, 8, 128), F32)
            ff[3 + c, 0] = jnp.zeros((9, 8, 128), F32)

        def load_fine(x, carry):
            ok = inside & (inside_x(x) + jnp.zeros((8, 128), jnp.int32) > 0)
            for c in range(9):
                for ry in range(3):
                    for r, here in enumerate(gather_in(stage, (c, x), ry)):
                        if 3 <= c < 6:
                            ff[c, x + 1, 3 * ry + r] = jnp.where(ok, 2.0 * here, 0.0)
                        else:
                            ff[c, x, 3 * ry + r] = jnp.where(ok, here, 0.0)
            return carry

        lax.fori_loop(0, 6, load_fine, 0)

        back_y, back_z = (8 - y0 % 8) % 8, (128 - z0 % 128) % 128
        lat_copy(STEPS).wait_recv()
        for c in range(3):
            for i in range(2):
                ear[0, c, i] = pltpu.roll(pltpu.roll(lat_r[STEPS, c, i], back_y, 0), back_z, 1)

        edge_y = {0: rows == 0, 2: rows == ly - 1}
        edge_z = {0: lanes == 0, 2: lanes == lz - 1}

        def at_layer(x, carry):
            ok = inside & (inside_x(x) + jnp.zeros((8, 128), jnp.int32) > 0)
            edge = jnp.where((x == 0) | (x == 3 * lx - 1), 1, 0).astype(jnp.int32)
            edge_x = ok & (edge + jnp.zeros((8, 128), jnp.int32) > 0)
            ok_y = {q: m & ok for q, m in edge_y.items()}
            ok_z = {q: m & ok for q, m in edge_z.items()}
            xc = x // 3
            for ry in range(3):
                for rz in range(3):
                    t = 3 * ry + rz
                    ex, ey, ez = ff[0, x, t], ff[1, x, t], ff[2, x, t]
                    if ry < 2:
                        exy, ezy = ff[0, x, t + 3], ff[2, x, t + 3]
                    else:
                        exy, ezy = yfwd(ff[0, x, rz]), yfwd(ff[2, x, rz])
                    if rz < 2:
                        exz, eyz = ff[0, x, t + 1], ff[1, x, t + 1]
                    else:
                        exz, eyz = zfwd(ff[0, x, 3 * ry]), zfwd(ff[1, x, 3 * ry])
                    eyx, ezx = ff[1, x + 1, t], ff[2, x + 1, t]
                    ff[3, x + 1, t] = ff[3, x + 1, t] - ((ezy - ez) - (eyz - ey))
                    ff[4, x + 1, t] = ff[4, x + 1, t] - ((exz - ex) - (ezx - ez))
                    ff[5, x + 1, t] = ff[5, x + 1, t] - ((eyx - ey) - (exy - ex))
            for ry in range(3):
                for rz in range(3):
                    t = 3 * ry + rz
                    hx, hy, hz = ff[3, x + 1, t], ff[4, x + 1, t], ff[5, x + 1, t]
                    if ry > 0:
                        hxy, hzy = ff[3, x + 1, t - 3], ff[5, x + 1, t - 3]
                    else:
                        hxy, hzy = ybwd(ff[3, x + 1, 6 + rz]), ybwd(ff[5, x + 1, 6 + rz])
                    if rz > 0:
                        hxz, hyz = ff[3, x + 1, t - 1], ff[4, x + 1, t - 1]
                    else:
                        hxz, hyz = zbwd(ff[3, x + 1, 3 * ry + 2]), zbwd(ff[4, x + 1, 3 * ry + 2])
                    hyx, hzx = ff[4, x, t], ff[5, x, t]
                    curls = ((hz - hzy) - (hy - hyz), (hx - hxz) - (hz - hzx), (hy - hyx) - (hx - hxy))
                    ka, kc, kb, kf, kg = (fk[q, x, t] for q in range(5))
                    for c in range(3):
                        pol = ff[6 + c, x, t]
                        new = ka * ff[c, x, t] + kc * curls[c] + kb * pol
                        marks = []
                        if c != 0:
                            marks.append(edge_x)
                        if c != 1 and ry in ok_y:
                            marks.append(ok_y[ry])
                        if c != 2 and rz in ok_z:
                            marks.append(ok_z[rz])
                        if marks:
                            new = jnp.where(functools.reduce(jnp.logical_or, marks), drv[c, xc], new)
                        ff[c, x, t] = new
                        ff[6 + c, x, t] = kf * pol + kg * new
            return carry

        def fine_step(n, carry):
            lat_copy(n).wait_recv()
            for c in range(3):
                for i in range(2):
                    ear[1, c, i] = pltpu.roll(pltpu.roll(lat_r[n, c, i], back_y, 0), back_z, 1)

            def substep(s, carry):
                weight = (s + 1).astype(F32) * (1.0 / 3.0)
                drv[...] = ear[0] + weight * (ear[1] - ear[0])
                return lax.fori_loop(0, 6, at_layer, carry)

            lax.fori_loop(0, 3, substep, 0)
            for i in range(2):
                ok = inside & (inside_x(3 * i) + jnp.zeros((8, 128), jnp.int32) > 0)
                for c in range(3):
                    total = functools.reduce(
                        jnp.add, [ff[c, 3 * i + j, t] for j in range(3) for t in range(9)])
                    latest = ear[1, c, i]
                    delta = jnp.where(ok, total * (1.0 / 27.0) - latest, 0.0)
                    ear[0, c, i] = latest + delta
                    del_s[n, c, i] = pltpu.roll(pltpu.roll(delta, y0 % 8, 0), z0 % 128, 1)
            del_copy(n).start()
            return carry

        lax.fori_loop(0, STEPS, fine_step, 0)

        def save_fine(x, carry):
            for c in range(9):
                for ry in range(3):
                    lift = 1 if 3 <= c < 6 else 0
                    parts = [ff[c, x + lift, 3 * ry + r] for r in range(3)]
                    for v in range(3):
                        got = [pick(part, third[v]) for part in parts]
                        value = jnp.where(phase[v] == 0, got[0], jnp.where(phase[v] == 1, got[1], got[2]))
                        if lift:
                            value = 0.5 * value
                        stage[v, c, x, pl.ds(ry, 8, stride=3), :] = value
            return carry

        lax.fori_loop(0, 6, save_fine, 0)
        f_out = [pltpu.make_async_copy(stage.at[v], out.at[0, :, :, :, pl.ds(128 * v, 128)], lsem.at[v]) for v in range(3)]
        for cp in f_out:
            cp.start()
        for n in range(STEPS):
            del_copy(n).wait_send()
        for cp in f_out:
            cp.wait()


def solution(mesh):
    nx, ny = mesh.shape["gx"], mesh.shape["gy"]

    def body(fields, material, permit, conduct, relax, debye, subgrids):
        vm = pltpu.VMEM
        dma = pltpu.SemaphoreType.DMA
        slots = [
            vm((STEPS, 2, 24, 384), F32), vm((STEPS, 2, 8, 384), F32),
            vm((STEPS, 2, 24, 384), F32), vm((STEPS, 2, 8, 384), F32),
            vm((STEPS, 8, 384), F32), vm((STEPS, 8, 384), F32),
        ]
        region = (3, 2, 8, 128)
        return pl.pallas_call(
            functools.partial(kernel, nx, ny),
            out_shape=jax.ShapeDtypeStruct(fields.shape, F32),
            in_specs=[pl.BlockSpec(memory_space=pl.ANY)] * 2 + [pl.BlockSpec(memory_space=pltpu.SMEM)] * 5,
            out_specs=pl.BlockSpec(memory_space=pl.ANY),
            scratch_shapes=[
                vm((3, 7, 32, 384), F32), vm((3, 7, 32, 384), F32), vm((3, 6, 24, 384), F32), vm((5, 6, 24, 384), F32),
                vm((3, 9, 6, 24, 128), F32), vm((3, 6, 24, 128), jnp.int32),
                vm((9, 7, 9, 8, 128), F32), vm((5, 6, 9, 8, 128), F32),
                vm((5, 16, 384), F32), vm((2, 8, 384), F32), vm((2,) + region, F32), vm(region, F32),
                *slots, *slots,
                vm((STEPS + 1,) + region, F32), vm((STEPS + 1,) + region, F32),
                vm((STEPS,) + region, F32), vm((STEPS,) + region, F32),
                dma((6,)), dma((6, STEPS)), dma((6, STEPS)),
                dma((STEPS + 1,)), dma((STEPS + 1,)), dma((STEPS,)), dma((STEPS,)),
            ],
            compiler_params=pltpu.CompilerParams(
                collective_id=0, has_side_effects=True, vmem_limit_bytes=40 * 1024 * 1024),
        )(fields, material, permit, conduct, relax, debye, subgrids)

    return jax.shard_map(
        body,
        mesh=mesh,
        in_specs=(P("grid", None, "gx", "gy", None), P("grid", "gx", "gy", None), P(), P(), P(), P(), P("gx", "gy", None)),
        out_specs=P("grid", None, "gx", "gy", None),
        check_vma=False,
    )
```

time: 672 us -> 61.3 us (0.09); the launches traced: 659 us -> 60.8 us
  waiting for transfers between devices: 470 us -> 0 us
  other arithmetic: 61.9 us -> 0 us
  Pallas kernels: 0 us -> 53.7 us
  starting transfers between devices: 40.7 us -> 0 us
  loops' own time: 35.8 us -> 0 us
  local copies, waits for them, and re-layouts: 42.3 us -> 7.04 us
  between operations: 8.4 us -> 0.02 us
    ppermute x18 -> x0, waiting for transfers between devices: 470 us -> none  [shifted(): return lax.ppermute(value, axis, pairs)]
    pallas_call x0 -> x1, Pallas kernels: none -> 53.7 us  [body(): pl.pallas_call(functools.partial(kernel, nx, ny), out_shape=jax.ShapeDtyp...]
    ppermute x18 -> x0, starting transfers between devices: 40.7 us -> none  [shifted(): return lax.ppermute(value, axis, pairs)]
    another operation x25 -> x0, loops' own time: 35.8 us -> none  [the longest x3 18.8 us: body(): lax.cond(coarse, lambda: jnp.zeros_like(earlier), lambda: restrict(local[...]
    div x2 -> x0, other arithmetic: 20.4 us -> none  [the longest x1 10.2 us: material_factors(): (1.0 - damping) / (1.0 + damping)]
    slice x26 -> x0, local copies, waits for them, and re-layouts: 20.1 us -> none  [the longest x3 5.1 us: coarse_step(): efield, hfield, polarization = (local[0:3], local[3:6], local[6:9])]
    concatenate x9 -> x0, other arithmetic: 12.1 us -> none  [the longest x3 4.86 us: coarse_step(): return jnp.concatenate([efield, hfield, polarization])]
    select_n x3 -> x0, other arithmetic: 8.27 us -> none  [the longest x1 5.26 us: lookup(): picked = jnp.where(material == candidate, entries[candidate], picked)]
  transfers between devices with their start and end apart: 18 -> 0, of which waited for: 11 -> 0; matrix products, arithmetic and copies ran while one was open for 7% -> 0% of each run, Pallas kernels for 0% -> 0%
where the time goes in v1:
time: 61.3 us; the launch traced here: 60.8 us
  Pallas kernels  53.7 us (88%)
  local copies, waits for them, and re-layouts  7.04 us (11%)
    pallas_call x1, Pallas kernels, body(): pl.pallas_call(functools.partial(kernel, nx, ny), out_shape=jax.ShapeDtyp...  53.7 us
    unnamed x15, local copies, waits for them, and re-layouts  7.04 us

profile of v1, /device:TPU:40, one launch (start us, length us, event | category | flops | bytes accessed | tf_op | source)
XLA Modules:
  0.0 60.8 jit_solution(79611864626542582)
XLA Ops:
  0.0 0.0 copy-start
  0.0 1.6 %copy-done = f32[1,9,6,24,384]{4,3,2,1,0:T(8,128)S(1)} copy-done((f32[1,9,6,24,384]{4,3,2,1,0:T(8,128)S(1)}, f32[1,9,6,24,384]{4,3,2,1,0:T(8,128)}, u32[]{:S(2)}) %copy-start) | copy-done | bytes 1990680
  1.6 0.0 copy-start.1
  1.6 0.9 %copy-done.1 = s32[1,6,24,384]{3,2,1,0:T(8,128)S(1)} copy-done((s32[1,6,24,384]{3,2,1,0:T(8,128)S(1)}, s32[1,6,24,384]{3,2,1,0:T(8,128)}, u32[]{:S(2)}) %copy-start.1) | copy-done | bytes 221208
  2.5 0.0 copy-start.2
  2.5 0.7 %copy-done.2 = f32[8]{0:T(128)S(1)} copy-done((f32[8]{0:T(128)S(1)}, f32[8]{0:T(128)}, u32[]{:S(2)}) %copy-start.2) | copy-done | bytes 56
  3.1 0.0 copy-start.3
  3.1 0.7 %copy-done.3 = f32[8]{0:T(128)S(1)} copy-done((f32[8]{0:T(128)S(1)}, f32[8]{0:T(128)}, u32[]{:S(2)}) %copy-start.3) | copy-done | bytes 56
  3.8 0.0 copy-start.4
  3.8 0.7 %copy-done.4 = f32[8]{0:T(128)S(1)} copy-done((f32[8]{0:T(128)S(1)}, f32[8]{0:T(128)}, u32[]{:S(2)}) %copy-start.4) | copy-done | bytes 56
  4.5 0.0 copy-start.5
  4.5 0.7 %copy-done.5 = f32[8]{0:T(128)S(1)} copy-done((f32[8]{0:T(128)S(1)}, f32[8]{0:T(128)}, u32[]{:S(2)}) %copy-start.5) | copy-done | bytes 56
  5.1 0.0 copy-start.6
  5.1 0.7 %copy-done.6 = s32[1,1,6]{2,1,0:T(1,128)S(1)} copy-done((s32[1,1,6]{2,1,0:T(1,128)S(1)}, s32[1,1,6]{2,1,0:T(1,128)}, u32[]{:S(2)}) %copy-start.6) | copy-done | bytes 48
  5.8 53.7 %shard_map.73 = f32[1,9,6,24,384]{4,3,2,1,0:T(8,128)S(1)} custom-call(f32[1,9,6,24,384]{4,3,2,1,0:T(8,128)S(1)} %copy-done, s32[1,6,24,384]{3,2,1,0:T(8,128)S(1)} %copy-done.1, f32[8]{0:T(128)S(1)} %copy-done.2, f32[8]{0:T(128)S(1)} %copy-done.3, f32[8]{0:T(128)S(1)} %copy-done.4, f32[8]{0:T(128)S(1)} %copy-done.5, s32[1,1,6]{2,1,0:T(1,128)S(1)} %copy-done.6), custom_call_target="tpu_custom_call" | custom-call | tf_op jit(solution)/shard_map/pallas_call | solution.py:486
  59.5 1.3 %copy.9 = f32[1,9,6,24,384]{4,3,2,1,0:T(8,128)} copy(f32[1,9,6,24,384]{4,3,2,1,0:T(8,128)S(1)} %shard_map.73) | data formatting | bytes 3981312
Async XLA Ops:
  0.0 1.6 %copy-start = (f32[1,9,6,24,384]{4,3,2,1,0:T(8,128)S(1)}, f32[1,9,6,24,384]{4,3,2,1,0:T(8,128)}, u32[]{:S(2)}) copy-start(f32[1,9,6,24,384]{4,3,2,1,0:T(8,128)} %fields.1) | copy-start | bytes 5971972
  1.6 0.9 %copy-start.1 = (s32[1,6,24,384]{3,2,1,0:T(8,128)S(1)}, s32[1,6,24,384]{3,2,1,0:T(8,128)}, u32[]{:S(2)}) copy-start(s32[1,6,24,384]{3,2,1,0:T(8,128)} %material.1) | copy-start | bytes 663556
  2.5 0.7 %copy-start.2 = (f32[8]{0:T(128)S(1)}, f32[8]{0:T(128)}, u32[]{:S(2)}) copy-start(f32[8]{0:T(128)} %permit.1) | copy-start | bytes 100
  3.1 0.7 %copy-start.3 = (f32[8]{0:T(128)S(1)}, f32[8]{0:T(128)}, u32[]{:S(2)}) copy-start(f32[8]{0:T(128)} %conduct.1) | copy-start | bytes 100
  3.8 0.7 %copy-start.4 = (f32[8]{0:T(128)S(1)}, f32[8]{0:T(128)}, u32[]{:S(2)}) copy-start(f32[8]{0:T(128)} %relax.1) | copy-start | bytes 100
  4.5 0.7 %copy-start.5 = (f32[8]{0:T(128)S(1)}, f32[8]{0:T(128)}, u32[]{:S(2)}) copy-start(f32[8]{0:T(128)} %debye.1) | copy-start | bytes 100
  5.1 0.7 %copy-start.6 = (s32[1,1,6]{2,1,0:T(1,128)S(1)}, s32[1,1,6]{2,1,0:T(1,128)}, u32[]{:S(2)}) copy-start(s32[1,1,6]{2,1,0:T(1,128)} %subgrids.1) | copy-start | bytes 76

commit v2 on v1

v2 whole, which is shorter than its diff:
```python
import functools

import jax
import jax.numpy as jnp
from jax import lax
from jax.experimental import pallas as pl
from jax.experimental.pallas import tpu as pltpu
from jax.sharding import PartitionSpec as P

MESH = pl.DeviceIdType.MESH
STEPS = 3
F32 = jnp.float32

TO_NEXT = ((-1, 0), (0, -1), (1, 0), (0, 1), (1, -1), (-1, 1))
XE, YE, XG, YG, C1, C2 = range(6)


def lane_iota():
    return lax.broadcasted_iota(jnp.int32, (8, 128), 1)


def row_iota():
    return lax.broadcasted_iota(jnp.int32, (8, 128), 0)


def pick(tile, index):
    return jnp.take_along_axis(tile, index, axis=1, mode="promise_in_bounds")


def zfwd(v):
    n = v.shape[-1]
    lanes = lax.broadcasted_iota(jnp.int32, v.shape, v.ndim - 1)
    return jnp.where(lanes == n - 1, 0.0, pltpu.roll(v, n - 1, v.ndim - 1))


def zbwd(v):
    lanes = lax.broadcasted_iota(jnp.int32, v.shape, v.ndim - 1)
    return jnp.where(lanes == 0, 0.0, pltpu.roll(v, 1, v.ndim - 1))


def yfwd(t):
    return jnp.where(row_iota() == 7, 0.0, pltpu.roll(t, 7, 0))


def ybwd(t):
    return jnp.where(row_iota() == 0, 0.0, pltpu.roll(t, 1, 0))


def tables(permit, conduct, relax, debye, factor, courant):
    lane = lane_iota()

    def spread(ref):
        out = jnp.ones((8, 128), F32)
        for m in range(8):
            out = jnp.where(lane == m, ref[m], out)
        return out

    eps = spread(permit)
    damping = spread(conduct) * factor / (2.0 * eps)
    f0 = (1.0 - damping) / (1.0 + damping)
    f1 = 1.0 / (eps * (1.0 + damping))
    f2 = spread(relax) * factor
    f3 = jnp.exp(-f2)
    f4 = spread(debye)
    return f0 - f1 * f2 * f4, courant * f1, f1 * f2, f3, (1.0 - f3) * f4


def kernel(
    nx, ny,
    fields, material, permit, conduct, relax, debye, subgrids, out,
    e2, h2, p2, k, stage, mat, ff, fk, pk, pln, own, dl, pd, ear, drv, fkr,
    xe_s, ye_s, xg_s, yg_s, c1_s, c2_s,
    xe_r, ye_r, xg_r, yg_r, c1_r, c2_r,
    lat_s, lat_r, ini_s, ini_r, del_s, del_r,
    nx_s, ny_s, nd_s, nx_r, ny_r, nd_r, pos_s, pos_r, place_of,
    lsem, hs, hr, bs, br, ds, dr, ns, nr, ps, pr,
):
    grid = lax.axis_index("grid")
    ga = lax.axis_index("gx")
    gb = lax.axis_index("gy")
    coarse = grid == 0
    x0, y0, z0 = subgrids[0, 0, 0], subgrids[0, 0, 1], subgrids[0, 0, 2]
    lx, ly, lz = subgrids[0, 0, 3], subgrids[0, 0, 4], subgrids[0, 0, 5]
    sends = (xe_s, ye_s, xg_s, yg_s, c1_s, c2_s)
    recvs = (xe_r, ye_r, xg_r, yg_r, c1_r, c2_r)
    delta_s = (nx_s.at[0], ny_s.at[0], nx_s.at[1], ny_s.at[1], nd_s.at[0], nd_s.at[1])
    delta_r = (nx_r.at[0], ny_r.at[0], nx_r.at[1], ny_r.at[1], nd_r.at[0], nd_r.at[1])

    def exists(dx, dy):
        return (ga + dx >= 0) & (ga + dx < nx) & (gb + dy >= 0) & (gb + dy < ny)

    def device(g, dx, dy):
        return (g, jnp.clip(ga + dx, 0, nx - 1), jnp.clip(gb + dy, 0, ny - 1))

    partner = (1 - grid, ga, gb)
    rows, lanes = row_iota(), lane_iota()

    e_in = pltpu.make_async_copy(fields.at[0, 0:3], e2.at[0, :, 0:6, 0:24, :], lsem.at[0])
    h_in = pltpu.make_async_copy(fields.at[0, 3:6], h2.at[0, :, 1:7, 8:32, :], lsem.at[1])
    p_in = pltpu.make_async_copy(fields.at[0, 6:9], p2.at[0], lsem.at[2])
    f_in = [pltpu.make_async_copy(fields.at[0, :, :, :, pl.ds(128 * v, 128)], stage.at[v], lsem.at[v]) for v in range(3)]
    m_in = [pltpu.make_async_copy(material.at[0, :, :, pl.ds(128 * v, 128)], mat.at[v], lsem.at[3 + v]) for v in range(3)]

    @pl.when(coarse)
    def _():
        for cp in (e_in, h_in, p_in):
            cp.start()

    @pl.when(jnp.logical_not(coarse))
    def _():
        for cp in f_in:
            cp.start()

    for cp in m_in:
        cp.start()
    for ref in (nx_r, ny_r, nd_r, pos_r):
        ref[...] = jnp.zeros_like(ref)

    @pl.when(coarse)
    def _():
        for ref in (ye_s, yg_s, pk, pln, own) + recvs:
            ref[...] = jnp.zeros_like(ref)

    barrier = pltpu.get_barrier_semaphore()
    pl.semaphore_signal(barrier, inc=1, device_id=partner, device_id_type=MESH)
    count = jnp.int32(1)
    for dx, dy in TO_NEXT:
        count = count + exists(dx, dy).astype(jnp.int32)

        @pl.when(exists(dx, dy))
        def _():
            pl.semaphore_signal(barrier, inc=1, device_id=(grid, ga + dx, gb + dy), device_id_type=MESH)

    pos_s[...] = jnp.where(rows == 0, x0, jnp.where(rows == 1, y0, z0))
    pl.semaphore_wait(barrier, count)

    def remote(src, dst, send, recv, target):
        return pltpu.make_async_remote_copy(
            src_ref=src, dst_ref=dst, send_sem=send, recv_sem=recv, device_id=target, device_id_type=MESH)

    def halo_copy(m, n):
        return remote(sends[m].at[n], recvs[m].at[n], hs.at[m, n], hr.at[m, n], device(grid, *TO_NEXT[m]))

    def lat_copy(n):
        return remote(lat_s.at[n], lat_r.at[n], bs.at[n], br.at[n], partner)

    def ini_copy():
        return remote(ini_s, ini_r, bs.at[STEPS], br.at[STEPS], partner)

    def del_copy(n):
        return remote(del_s.at[n], del_r.at[n], ds.at[n], dr.at[n], partner)

    def near_copy(g, m, n):
        return remote(delta_s[m].at[n], delta_r[m].at[n], ns.at[g, m, n], nr.at[m, n], device(g, *TO_NEXT[m]))

    def pos_copy(m):
        return remote(pos_s, pos_r.at[m], ps.at[m], pr.at[m], device(grid, *TO_NEXT[m]))

    def each(turn, fun):
        for m, (dx, dy) in enumerate(TO_NEXT):
            @pl.when(exists(turn * dx, turn * dy))
            def _():
                fun(m)

    def learn_places():
        each(-1, lambda m: pos_copy(m).wait_recv())
        cp = pltpu.make_async_copy(pos_r, place_of, lsem.at[6])
        cp.start()
        cp.wait()

    def row_in(low, u):
        return (rows + 8 * u >= low) & (rows + 8 * u < low + 8)

    def lane_in(low, v):
        return (lanes + 128 * v >= low) & (lanes + 128 * v < low + 128)

    def tile_at(u, v):
        return (slice(8 * u, 8 * u + 8), slice(128 * v, 128 * v + 128))

    @pl.when(coarse)
    def _():
        flag_x = jnp.where(ga > 0, 1.0, 0.0).astype(F32)
        flag_y = jnp.where(gb > 0, 1.0, 0.0).astype(F32)
        row_ok = [row_in(y0, u) for u in range(3)]
        lane_ok = [lane_in(z0, v) for v in range(3)]
        wide = lax.broadcasted_iota(jnp.int32, (24, 384), 0)
        plane = lax.broadcasted_iota(jnp.int32, (8, 384), 0)

        def cut(load, i):
            tile = jnp.zeros((8, 128), F32)
            for u in range(3):
                for v in range(3):
                    tile = jnp.where(row_ok[u] & lane_ok[v], load(x0 + i, *tile_at(u, v)), tile)
            return tile

        def cut_latest(n, e):
            for i in range(2):
                for c in range(3):
                    lat_s[n, c, i] = cut(lambda x, r, l: e[c, x, r, l], i)
            lat_copy(n).start()

        def place(n, e):
            def at_x(x, carry):
                s0 = jnp.where(x == x0, 1.0, 0.0).astype(F32)
                s1 = jnp.where(x == x0 + 1, 1.0, 0.0).astype(F32)
                for c in range(3):
                    tile = s0 * del_r[n, c, 0] + s1 * del_r[n, c, 1]
                    for u in range(3):
                        for v in range(3):
                            spot = (c, x) + tile_at(u, v)
                            e[spot] = e[spot] + jnp.where(row_ok[u] & lane_ok[v], tile, 0.0)
                return carry

            lax.fori_loop(0, 6, at_x, 0)

        def send_halos(n, e, h):
            for x in range(6):
                ye_s[n, 0, x:x + 1, :] = e[0, x, 0:1, :]
                ye_s[n, 1, x:x + 1, :] = e[2, x, 0:1, :]
                for c in range(3):
                    pk[c, x:x + 1, :] = e[c, x, 23:24, :]
                pk[3, x:x + 1, :] = h[0, x + 1, 31:32, :]
                pk[4, x:x + 1, :] = h[2, x + 1, 31:32, :]
            xe_s[n] = e[1:3, 0, 0:24, :]
            ex, ey, ez = e[0, 5, 0:24, :], e[1, 5, 0:24, :], e[2, 5, 0:24, :]
            exy = jnp.where(wide == 23, 0.0, e[0, 5, 1:25, :])
            xg_s[n, 0] = h[1, 6, 8:32, :] - 0.5 * (zfwd(ex) - ex + ez)
            xg_s[n, 1] = h[2, 6, 8:32, :] + 0.5 * (ey + exy - ex)
            px, py, pz = pk[0, 0:8, :], pk[1, 0:8, :], pk[2, 0:8, :]
            yg_s[n, 0] = pk[3, 0:8, :] + 0.5 * (pz + zfwd(py) - py)
            yg_s[n, 1] = pk[4, 0:8, :] - 0.5 * (pk[1, 1:9, :] - py + px)
            c1_s[n] = jnp.broadcast_to(e[0, 5, 0:1, :], (8, 384))
            c2_s[n] = jnp.broadcast_to(e[1, 0, 23:24, :], (8, 384))
            each(1, lambda m: halo_copy(m, n).start())

        def put_halos(n, e, h):
            e[1:3, 6, 0:24, :] = xe_r[n]
            h[1, 0, 8:32, :] = flag_x * (xg_r[n, 0] + 0.5 * e[2, 0, 0:24, :])
            corner = jnp.where(wide == 23, jnp.broadcast_to(c1_r[n, 0:1, :], (24, 384)), 0.0)
            h[2, 0, 8:32, :] = flag_x * (xg_r[n, 1] - 0.5 * (e[1, 0, 0:24, :] - corner))
            for x in range(6):
                own[0, x:x + 1, :] = e[0, x, 0:1, :]
                own[1, x:x + 1, :] = e[2, x, 0:1, :]
            pln[0] = flag_y * (yg_r[n, 0] - 0.5 * own[1])
            pln[1] = flag_y * (yg_r[n, 1] + 0.5 * (own[0] - jnp.where(plane == 5, c2_r[n], 0.0)))
            for x in range(6):
                e[0, x, 24:25, :] = ye_r[n, 0, x:x + 1, :]
                e[2, x, 24:25, :] = ye_r[n, 1, x:x + 1, :]
                h[0, x + 1, 7:8, :] = pln[0, x:x + 1, :]
                h[2, x + 1, 7:8, :] = pln[1, x:x + 1, :]

        def mend_halos(n):
            d = n - 1
            each(-1, lambda m: near_copy(0, m, d).wait_recv())
            for u in range(3):
                for v in range(3):
                    spot = tile_at(u, v)
                    ok = row_in(place_of[XE, 1, 0], u) & lane_in(place_of[XE, 2, 0], v)
                    for q in range(2):
                        xe_r[(n, q) + spot] = xe_r[(n, q) + spot] + jnp.where(ok, nx_r[0, d, 1 + q], 0.0)
                    ok = row_in(place_of[XG, 1, 0], u) & lane_in(place_of[XG, 2, 0], v)
                    for c in range(3):
                        dl[(c,) + spot] = jnp.where(ok, nx_r[1, d, c], 0.0)
            tx, ty, tz = dl[0, 0:24, :], dl[1, 0:24, :], dl[2, 0:24, :]
            dl[0, 24:32, :] = jnp.zeros((8, 384), F32)
            xg_r[n, 0] = xg_r[n, 0] - 0.5 * (zfwd(tx) - tx + tz)
            xg_r[n, 1] = xg_r[n, 1] + 0.5 * (ty + dl[0, 1:25, :] - tx)
            for m, keep in ((YE, ny_r.at[0]), (YG, ny_r.at[1])):
                at = place_of[m, 0, 0]
                for c in range(3):
                    two = [jnp.broadcast_to(keep[d, 2 * c + i:2 * c + i + 1, :], (8, 128)) for i in range(2)]
                    both = jnp.where(rows == at, two[0], jnp.where(rows == at + 1, two[1], 0.0))
                    for v in range(3):
                        pd[c, :, 128 * v:128 * v + 128] = jnp.where(lane_in(place_of[m, 2, 0], v), both, 0.0)
                if m == YE:
                    ye_r[n, 0] = ye_r[n, 0] + pd[0]
                    ye_r[n, 1] = ye_r[n, 1] + pd[2]
                else:
                    yg_r[n, 0] = yg_r[n, 0] + 0.5 * (pd[2] + zfwd(pd[1]) - pd[1])
                    yg_r[n, 1] = yg_r[n, 1] - 0.5 * (pltpu.roll(pd[1], 7, 0) - pd[1] + pd[0])
            for m, ref, keep in ((C1, c1_r, nd_r.at[0]), (C2, c2_r, nd_r.at[1])):
                for v in range(3):
                    spot = (n, slice(0, 8), slice(128 * v, 128 * v + 128))
                    ref[spot] = ref[spot] + jnp.where(lane_in(place_of[m, 2, 0], v), keep[d], 0.0)

        def update(e, h, p, ed, hd, pd_):
            def at_x(x, carry):
                for u in range(3):
                    r = slice(8 * u, 8 * u + 8)
                    ra = slice(8 * u + 1, 8 * u + 9)
                    rh = slice(8 * u + 8, 8 * u + 16)
                    rb = slice(8 * u + 7, 8 * u + 15)
                    ex, ey, ez = e[0, x, r, :], e[1, x, r, :], e[2, x, r, :]
                    hx = h[0, x + 1, rh, :] - 0.5 * ((e[2, x, ra, :] - ez) - (zfwd(ey) - ey))
                    hy = h[1, x + 1, rh, :] - 0.5 * ((zfwd(ex) - ex) - (e[2, x + 1, r, :] - ez))
                    hz = h[2, x + 1, rh, :] - 0.5 * ((e[1, x + 1, r, :] - ey) - (e[0, x, ra, :] - ex))
                    hd[0, x + 1, rh, :] = hx
                    hd[1, x + 1, rh, :] = hy
                    hd[2, x + 1, rh, :] = hz
                    cx = (hz - hd[2, x + 1, rb, :]) - (hy - zbwd(hy))
                    cy = (hx - zbwd(hx)) - (hz - hd[2, x, rh, :])
                    cz = (hy - hd[1, x, rh, :]) - (hx - hd[0, x + 1, rb, :])
                    ka, kc, kb, kf, kg = (k[q, x, r, :] for q in range(5))
                    for c, (old, curl) in enumerate(((ex, cx), (ey, cy), (ez, cz))):
                        pol = p[c, x, r, :]
                        new = ka * old + kc * curl + kb * pol
                        ed[c, x, r, :] = new
                        if pd_ is not None:
                            pd_[c, x, r, :] = kf * pol + kg * new
                return carry

            lax.fori_loop(0, 6, at_x, 0)

        sets = [(e2.at[q], h2.at[q], p2.at[q]) for q in range(2)]
        each(1, lambda m: pos_copy(m).start())
        e_in.wait()
        h_in.wait()
        send_halos(0, sets[0][0], sets[0][1])
        for cp in m_in:
            cp.wait()
        tabs = tables(permit, conduct, relax, debye, 1.0, 0.5)

        def factors(x, carry):
            for u in range(3):
                for v in range(3):
                    here = mat[v, x, 8 * u:8 * u + 8, :]
                    for q in range(5):
                        k[(q, x) + tile_at(u, v)] = pick(tabs[q], here)
            return carry

        lax.fori_loop(0, 6, factors, 0)
        for i in range(2):
            for c in range(3):
                ini_s[c, i] = cut(lambda x, r, l: e2[0, c, x, r, l], i)
            for q in range(2):
                ini_s[3 + q, i] = cut(lambda x, r, l: k[q, x, r, l], i)
        ini_copy().start()
        p_in.wait()
        for n in range(STEPS):
            now, then = sets[n % 2], sets[(n + 1) % 2]
            each(-1, lambda m: halo_copy(m, n).wait_recv())
            if n == 0:
                put_halos(n, now[0], then[1])
                update(*now, *then)
                cut_latest(0, then[0])
                learn_places()
            else:
                put_halos(n, now[0], then[1])
                update(*now, then[0], then[1], None)
                cut_latest(n, then[0])
                del_copy(n - 1).wait_recv()
                place(n - 1, now[0])
                mend_halos(n)
                put_halos(n, now[0], then[1])
                update(*now, *then)
            if n + 1 < STEPS:
                send_halos(n + 1, then[0], then[1])
        e, h, p = sets[STEPS % 2]
        h_out = pltpu.make_async_copy(h.at[:, 1:7, 8:32, :], out.at[0, 3:6], lsem.at[1])
        p_out = pltpu.make_async_copy(p, out.at[0, 6:9], lsem.at[2])
        h_out.start()
        p_out.start()
        del_copy(STEPS - 1).wait_recv()
        place(STEPS - 1, e)
        e_out = pltpu.make_async_copy(e.at[:, 0:6, 0:24, :], out.at[0, 0:3], lsem.at[0])
        e_out.start()

        each(1, lambda m: pos_copy(m).wait_send())
        for n in range(STEPS):
            each(1, lambda m: halo_copy(m, n).wait_send())
            lat_copy(n).wait_send()
        ini_copy().wait_send()
        h_out.wait()
        p_out.wait()
        e_out.wait()

    @pl.when(jnp.logical_not(coarse))
    def _():
        none = jnp.zeros((8, 128), jnp.int32)
        inside = (rows < ly) & (lanes < lz)
        two = lx == 2

        def inside_x(x):
            return jnp.where((x < 3) | two, 1, 0).astype(jnp.int32)

        each(1, lambda m: pos_copy(m).start())
        tabs = tables(permit, conduct, relax, debye, 1.0 / 3.0, 0.25)
        spread = [3 * lanes + r for r in range(3)]
        packed = [(lanes + 128 * v) for v in range(3)]
        third = [q // 3 for q in packed]
        phase = [q - 3 * t for q, t in zip(packed, third)]

        def gather_in(ref, lead, ry):
            parts = [ref[(v,) + lead + (pl.ds(ry, 8, stride=3), slice(None))] for v in range(3)]
            tiles = []
            for r in range(3):
                at, src = spread[r] & 127, spread[r] >> 7
                got = [pick(part, at) for part in parts]
                tiles.append(jnp.where(src == 0, got[0], jnp.where(src == 1, got[1], got[2])))
            return tiles

        for cp in m_in:
            cp.wait()

        def fine_factors(x, carry):
            ok = inside & (inside_x(x) + none > 0)
            for ry in range(3):
                for r, here in enumerate(gather_in(mat, (x,), ry)):
                    ka, kc, kb, kf, kg = (pick(tabs[q], here) for q in range(5))
                    t = 3 * ry + r
                    fk[0, x, t] = ka
                    fk[1, x, t] = jnp.where(ok, kc, 0.0)
                    fk[2, x, t] = jnp.where(ok, kb * kg, 0.0)
                    fk[3, x, t] = kf
                    fk[4, x, t] = kg
                    fkr[x, t] = 1.0 / kg
            return carry

        lax.fori_loop(0, 6, fine_factors, 0)
        for cp in f_in:
            cp.wait()
        for c in range(3):
            ff[c, 6] = jnp.zeros((9, 8, 128), F32)
            ff[3 + c, 0] = jnp.zeros((9, 8, 128), F32)

        def load_fine(x, carry):
            ok = inside & (inside_x(x) + none > 0)
            for c in range(9):
                for ry in range(3):
                    for r, here in enumerate(gather_in(stage, (c, x), ry)):
                        t = 3 * ry + r
                        if 3 <= c < 6:
                            ff[c, x + 1, t] = jnp.where(ok, 2.0 * here, 0.0)
                        elif c < 3:
                            ff[c, x, t] = jnp.where(ok, here, 0.0)
                        else:
                            ff[c, x, t] = jnp.where(ok, here * fkr[x, t], 0.0)
            return carry

        lax.fori_loop(0, 6, load_fine, 0)

        back_y, back_z = (8 - y0 % 8) % 8, (128 - z0 % 128) % 128

        def to_box(tile):
            return pltpu.roll(pltpu.roll(tile, back_y, 0), back_z, 1)

        def from_box(tile):
            return pltpu.roll(pltpu.roll(tile, y0 % 8, 0), z0 % 128, 1)

        edge_y = {0: rows == 0, 2: rows == ly - 1}
        edge_z = {0: lanes == 0, 2: lanes == lz - 1}

        def at_layer(x, carry):
            ok = inside & (inside_x(x) + none > 0)
            edge = jnp.where((x == 0) | (x == 3 * lx - 1), 1, 0).astype(jnp.int32)
            edge_x = ok & (edge + none > 0)
            ok_y = {q: m & ok for q, m in edge_y.items()}
            ok_z = {q: m & ok for q, m in edge_z.items()}
            xc = x // 3
            tiles = [(ry, rz) for ry in range(3) for rz in range(3)]
            E = {(c, t): ff[c, x, t] for c in range(3) for t in range(9)}
            F = {(c, t): ff[c, x + 1, t] for c in (1, 2) for t in range(9)}
            H = {}
            for ry, rz in tiles:
                t = 3 * ry + rz
                ex, ey, ez = (E[c, t] for c in range(3))
                if ry < 2:
                    exy, ezy = E[0, t + 3], E[2, t + 3]
                else:
                    exy, ezy = yfwd(E[0, rz]), yfwd(E[2, rz])
                if rz < 2:
                    exz, eyz = E[0, t + 1], E[1, t + 1]
                else:
                    exz, eyz = zfwd(E[0, 3 * ry]), zfwd(E[1, 3 * ry])
                H[0, t] = ff[3, x + 1, t] - ((ezy - ez) - (eyz - ey))
                H[1, t] = ff[4, x + 1, t] - ((exz - ex) - (F[2, t] - ez))
                H[2, t] = ff[5, x + 1, t] - ((F[1, t] - ey) - (exy - ex))
                for c in range(3):
                    ff[3 + c, x + 1, t] = H[c, t]
            for ry, rz in tiles:
                t = 3 * ry + rz
                hx, hy, hz = (H[c, t] for c in range(3))
                if ry > 0:
                    hxy, hzy = H[0, t - 3], H[2, t - 3]
                else:
                    hxy, hzy = ybwd(H[0, 6 + rz]), ybwd(H[2, 6 + rz])
                if rz > 0:
                    hxz, hyz = H[0, t - 1], H[1, t - 1]
                else:
                    hxz, hyz = zbwd(H[0, 3 * ry + 2]), zbwd(H[1, 3 * ry + 2])
                hyx, hzx = ff[4, x, t], ff[5, x, t]
                curls = ((hz - hzy) - (hy - hyz), (hx - hxz) - (hz - hzx), (hy - hyx) - (hx - hxy))
                ka, kc, kb, kf = (fk[q, x, t] for q in range(4))
                for c in range(3):
                    pol = ff[6 + c, x, t]
                    new = ka * E[c, t] + kc * curls[c] + kb * pol
                    marks = []
                    if c != 0:
                        marks.append(edge_x)
                    if c != 1 and ry in ok_y:
                        marks.append(ok_y[ry])
                    if c != 2 and rz in ok_z:
                        marks.append(ok_z[rz])
                    if marks:
                        new = jnp.where(functools.reduce(jnp.logical_or, marks), drv[c, xc], new)
                    ff[c, x, t] = new
                    ff[6 + c, x, t] = kf * pol + new
            return carry

        wrows = lax.broadcasted_iota(jnp.int32, (16, 256), 0)
        wlanes = lax.broadcasted_iota(jnp.int32, (16, 256), 1)
        at_y = y0 - 4 + ((wrows - (y0 - 4)) & 15)
        at_z = z0 - 64 + ((wlanes - (z0 - 64)) & 255)

        def w_in(at, low, size):
            return (at >= low) & (at < low + size)

        def twice(tile):
            return jnp.concatenate([jnp.concatenate([tile, tile], axis=1)] * 2, axis=0)

        def as_int(flag):
            return jnp.where(flag, 1, 0).astype(jnp.int32)

        def correction(n):
            each(-1, lambda m: near_copy(1, m, n - 1).wait_recv())
            d = n - 1
            region = w_in(at_y, y0, 8) & w_in(at_z, z0, 128)
            wide_none = jnp.zeros((16, 256), jnp.int32)
            w = {}
            for c in range(3):
                for xr in range(-1, 3):
                    w[c, xr] = jnp.where(region, twice(del_s[d, c, xr]), 0.0) if 0 <= xr < 2 else jnp.zeros((16, 256), F32)
            for m, xr, at_edge in ((XE, 2, x0 == 4), (XG, -1, x0 == 0)):
                ok = w_in(at_y, place_of[m, 1, 0], 8) & w_in(at_z, place_of[m, 2, 0], 128)
                ok = ok & (as_int(at_edge) + wide_none > 0)
                for c in range(3):
                    w[c, xr] = w[c, xr] + jnp.where(ok, twice(nx_r[m // 2, d, c]), 0.0)
            for m, y in ((YE, 24), (YG, -1)):
                ok = (at_y == y) & w_in(at_z, place_of[m, 2, 0], 128)
                for c in range(3):
                    two_rows = [ny_r[m // 2, d, 2 * c + i:2 * c + i + 1, :] for i in range(2)]
                    for xr in range(-1, 3):
                        i = x0 + xr - place_of[m, 0, 0]
                        s0 = jnp.where(i == 0, 1.0, 0.0).astype(F32)
                        s1 = jnp.where(i == 1, 1.0, 0.0).astype(F32)
                        row = jnp.broadcast_to(s0 * two_rows[0] + s1 * two_rows[1], (8, 128))
                        w[c, xr] = w[c, xr] + jnp.where(ok, twice(row), 0.0)
            for m, c, xr, y, at_edge in ((C1, 0, -1, 24, x0 == 0), (C2, 1, 2, -1, x0 == 4)):
                ok = (at_y == y) & w_in(at_z, place_of[m, 2, 0], 128) & (as_int(at_edge) + wide_none > 0)
                w[c, xr] = w[c, xr] + jnp.where(ok, twice(nd_r[m - 4, d]), 0.0)

            def up_y(a):
                return pltpu.roll(a, 15, 0)

            def up_z(a):
                return pltpu.roll(a, 255, 1)

            def down_y(a):
                return pltpu.roll(a, 1, 0)

            def down_z(a):
                return pltpu.roll(a, 1, 1)

            held = (at_z >= 0) & (at_y + 24 * gb >= 0)
            hh = {}
            for xr in range(-1, 2):
                ok = held & (as_int(x0 + xr + 6 * ga >= 0) + wide_none > 0)
                ex, ey, ez = (w[c, xr] for c in range(3))
                moved = ((up_y(ez) - ez) - (up_z(ey) - ey), (up_z(ex) - ex) - (w[2, xr + 1] - ez),
                         (w[1, xr + 1] - ey) - (up_y(ex) - ex))
                for c in range(3):
                    hh[c, xr] = jnp.where(ok, -0.5 * moved[c], 0.0)
            for xr in range(2):
                hx, hy, hz = (hh[c, xr] for c in range(3))
                curls = ((hz - down_y(hz)) - (hy - down_z(hy)), (hx - down_z(hx)) - (hz - hh[2, xr - 1]),
                         (hy - hh[1, xr - 1]) - (hx - down_y(hx)))
                for c in range(3):
                    kept = jnp.where(region, curls[c], 0.0)
                    tile = (kept[0:8, 0:128] + kept[0:8, 128:256]) + (kept[8:16, 0:128] + kept[8:16, 128:256])
                    ear[1, c, xr] = to_box(lat_r[n, c, xr] + ini_r[3, xr] * del_s[d, c, xr] + ini_r[4, xr] * tile)

        learn_places()
        ini_copy().wait_recv()
        for c in range(3):
            for i in range(2):
                ear[0, c, i] = to_box(ini_r[c, i])

        for n in range(STEPS):
            lat_copy(n).wait_recv()
            if n == 0:
                for c in range(3):
                    for i in range(2):
                        ear[1, c, i] = to_box(lat_r[0, c, i])
            else:
                correction(n)

            def substep(s, carry):
                weight = (s + 1).astype(F32) * (1.0 / 3.0)
                drv[...] = ear[0] + weight * (ear[1] - ear[0])
                return lax.fori_loop(0, 6, at_layer, carry)

            lax.fori_loop(0, 3, substep, 0)
            for i in range(2):
                ok = inside & (inside_x(3 * i) + none > 0)
                for c in range(3):
                    total = functools.reduce(
                        jnp.add, [ff[c, 3 * i + j, t] for j in range(3) for t in range(9)])
                    latest = ear[1, c, i]
                    delta = jnp.where(ok, total * (1.0 / 27.0) - latest, 0.0)
                    ear[0, c, i] = latest + delta
                    del_s[n, c, i] = from_box(delta)
            if n + 1 < STEPS:
                low, high = (jnp.where(x0 == q, 1.0, 0.0).astype(F32) for q in (0, 4))
                left, right = (jnp.where(y0 == q, 1.0, 0.0).astype(F32) for q in (0, 16))
                for c in range(3):
                    nx_s[0, n, c] = low * del_s[n, c, 0]
                    nx_s[1, n, c] = high * del_s[n, c, 1]
                    for i in range(2):
                        ny_s[0, n, 2 * c + i:2 * c + i + 1, :] = left * del_s[n, c, i, 0:1, :]
                        ny_s[1, n, 2 * c + i:2 * c + i + 1, :] = right * del_s[n, c, i, 7:8, :]
                for q in range(2):
                    ny_s[q, n, 6:8, :] = jnp.zeros((2, 128), F32)
                nd_s[0, n] = jnp.broadcast_to((high * left) * del_s[n, 0, 1, 0:1, :], (8, 128))
                nd_s[1, n] = jnp.broadcast_to((low * right) * del_s[n, 1, 0, 7:8, :], (8, 128))
                each(1, lambda m: near_copy(1, m, n).start())
                del_copy(n).start()
                each(1, lambda m: near_copy(0, m, n).start())
            else:
                del_copy(n).start()

        def save_fine(x, carry):
            for c in range(9):
                for ry in range(3):
                    lift = 1 if 3 <= c < 6 else 0
                    parts = [ff[c, x + lift, 3 * ry + r] for r in range(3)]
                    if c >= 6:
                        parts = [part * fk[4, x, 3 * ry + r] for r, part in enumerate(parts)]
                    for v in range(3):
                        got = [pick(part, third[v]) for part in parts]
                        value = jnp.where(phase[v] == 0, got[0], jnp.where(phase[v] == 1, got[1], got[2]))
                        if lift:
                            value = 0.5 * value
                        stage[v, c, x, pl.ds(ry, 8, stride=3), :] = value
            return carry

        lax.fori_loop(0, 6, save_fine, 0)
        f_out = [pltpu.make_async_copy(stage.at[v], out.at[0, :, :, :, pl.ds(128 * v, 128)], lsem.at[v]) for v in range(3)]
        for cp in f_out:
            cp.start()
        each(1, lambda m: pos_copy(m).wait_send())
        for n in range(STEPS):
            del_copy(n).wait_send()
            if n + 1 < STEPS:
                for g in range(2):
                    each(1, lambda m: near_copy(g, m, n).wait_send())
        for cp in f_out:
            cp.wait()


def solution(mesh):
    nx, ny = mesh.shape["gx"], mesh.shape["gy"]

    def body(fields, material, permit, conduct, relax, debye, subgrids):
        vm = pltpu.VMEM
        dma = pltpu.SemaphoreType.DMA
        slots = [
            vm((STEPS, 2, 24, 384), F32), vm((STEPS, 2, 8, 384), F32),
            vm((STEPS, 2, 24, 384), F32), vm((STEPS, 2, 8, 384), F32),
            vm((STEPS, 8, 384), F32), vm((STEPS, 8, 384), F32),
        ]
        region = (3, 2, 8, 128)
        near = [vm((2, STEPS - 1, 3, 8, 128), F32), vm((2, STEPS - 1, 8, 128), F32), vm((2, STEPS - 1, 8, 128), F32)]
        return pl.pallas_call(
            functools.partial(kernel, nx, ny),
            out_shape=jax.ShapeDtypeStruct(fields.shape, F32),
            in_specs=[pl.BlockSpec(memory_space=pl.ANY)] * 2 + [pl.BlockSpec(memory_space=pltpu.SMEM)] * 5,
            out_specs=pl.BlockSpec(memory_space=pl.ANY),
            scratch_shapes=[
                vm((2, 3, 7, 32, 384), F32), vm((2, 3, 7, 32, 384), F32), vm((2, 3, 6, 24, 384), F32), vm((5, 6, 24, 384), F32),
                vm((3, 9, 6, 24, 128), F32), vm((3, 6, 24, 128), jnp.int32),
                vm((9, 7, 9, 8, 128), F32), vm((5, 6, 9, 8, 128), F32),
                vm((5, 16, 384), F32), vm((2, 8, 384), F32), vm((2, 8, 384), F32), vm((3, 32, 384), F32), vm((3, 8, 384), F32),
                vm((2,) + region, F32), vm(region, F32), vm((6, 9, 8, 128), F32),
                *slots, *slots,
                vm((STEPS,) + region, F32), vm((STEPS,) + region, F32), vm((5, 2, 8, 128), F32), vm((5, 2, 8, 128), F32),
                vm((STEPS,) + region, F32), vm((STEPS,) + region, F32),
                *near, *near, vm((8, 128), jnp.int32), vm((6, 8, 128), jnp.int32), pltpu.SMEM((6, 8, 128), jnp.int32),
                dma((7,)), dma((6, STEPS)), dma((6, STEPS)),
                dma((STEPS + 1,)), dma((STEPS + 1,)), dma((STEPS,)), dma((STEPS,)),
                dma((2, 6, STEPS)), dma((6, STEPS)), dma((6,)), dma((6,)),
            ],
            compiler_params=pltpu.CompilerParams(
                collective_id=0, has_side_effects=True, vmem_limit_bytes=63 * 1024 * 1024),
        )(fields, material, permit, conduct, relax, debye, subgrids)

    return jax.shard_map(
        body,
        mesh=mesh,
        in_specs=(P("grid", None, "gx", "gy", None), P("grid", "gx", "gy", None), P(), P(), P(), P(), P("gx", "gy", None)),
        out_specs=P("grid", None, "gx", "gy", None),
        check_vma=False,
    )
```

time: 61.3 us -> 45.1 us (0.74)
  Pallas kernels: 53.7 us -> 41.8 us
  local copies, waits for them, and re-layouts: 7.04 us -> 2.96 us
    pallas_call x1, Pallas kernels: 53.7 us -> 41.8 us  [body(): pl.pallas_call(functools.partial(kernel, nx, ny), out_shape=jax.ShapeDtyp...]
    unnamed x15 -> x1, local copies, waits for them, and re-layouts: 7.04 us -> 2.96 us
where the time goes in v2:
time: 45.1 us; the launch traced here: 44.7 us
  Pallas kernels  41.8 us (93%)
  local copies, waits for them, and re-layouts  2.96 us (7%)
    pallas_call x1, Pallas kernels, body(): pl.pallas_call(functools.partial(kernel, nx, ny), out_shape=jax.ShapeDtyp...  41.8 us
    unnamed x1, local copies, waits for them, and re-layouts  2.96 us

profile of v2, /device:TPU:40, one launch (start us, length us, event | category | flops | bytes accessed | tf_op | source)
XLA Modules:
  0.0 44.7 jit_solution(17544893546204809747)
XLA Ops:
  0.0 41.8 %shard_map.73 = f32[1,9,6,24,384]{4,3,2,1,0:T(8,128)} custom-call(f32[1,9,6,24,384]{4,3,2,1,0:T(8,128)} %fields.1, s32[1,6,24,384]{3,2,1,0:T(8,128)} %material.1, f32[8]{0:T(128)} %permit.1, f32[8]{0:T(128)} %conduct.1, f32[8]{0:T(128)} %relax.1, f32[8]{0:T(128)} %debye.1, s32[1,1,6]{2,1,0:T(1,128)} %subgrids.1), custom_call_target="tpu_custom_call" | custom-call | tf_op jit(solution)/shard_map/pallas_call | solution.py:673
  41.8 3.0 %copy.9 = f32[1,9,6,24,384]{4,3,2,1,0:T(8,128)} copy(f32[1,9,6,24,384]{4,3,2,1,0:T(8,128)} %shard_map.73) | data formatting | bytes 3981312

commit v3 on v2

--- a/solution.py
+++ b/solution.py
@@ -132,7 +132,9 @@
             pl.semaphore_signal(barrier, inc=1, device_id=(grid, ga + dx, gb + dy), device_id_type=MESH)
 
     pos_s[...] = jnp.where(rows == 0, x0, jnp.where(rows == 1, y0, z0))
-    pl.semaphore_wait(barrier, count)
+
+    def all_here():
+        pl.semaphore_wait(barrier, count)
 
     def remote(src, dst, send, recv, target):
         return pltpu.make_async_remote_copy(
@@ -213,7 +215,7 @@
 
             lax.fori_loop(0, 6, at_x, 0)
 
-        def send_halos(n, e, h):
+        def pack_halos(n, e, h):
             for x in range(6):
                 ye_s[n, 0, x:x + 1, :] = e[0, x, 0:1, :]
                 ye_s[n, 1, x:x + 1, :] = e[2, x, 0:1, :]
@@ -231,6 +233,8 @@
             yg_s[n, 1] = pk[4, 0:8, :] - 0.5 * (pk[1, 1:9, :] - py + px)
             c1_s[n] = jnp.broadcast_to(e[0, 5, 0:1, :], (8, 384))
             c2_s[n] = jnp.broadcast_to(e[1, 0, 23:24, :], (8, 384))
+
+        def send_halos(n):
             each(1, lambda m: halo_copy(m, n).start())
 
         def put_halos(n, e, h):
@@ -309,13 +313,15 @@
                             pd_[c, x, r, :] = kf * pol + kg * new
                 return carry
 
-            lax.fori_loop(0, 6, at_x, 0)
+            lax.fori_loop(0, 6, at_x, 0, unroll=True)
 
         sets = [(e2.at[q], h2.at[q], p2.at[q]) for q in range(2)]
-        each(1, lambda m: pos_copy(m).start())
         e_in.wait()
         h_in.wait()
-        send_halos(0, sets[0][0], sets[0][1])
+        pack_halos(0, sets[0][0], sets[0][1])
+        all_here()
+        send_halos(0)
+        each(1, lambda m: pos_copy(m).start())
         for cp in m_in:
             cp.wait()
         tabs = tables(permit, conduct, relax, debye, 1.0, 0.5)
@@ -354,7 +360,8 @@
                 put_halos(n, now[0], then[1])
                 update(*now, *then)
             if n + 1 < STEPS:
-                send_halos(n + 1, then[0], then[1])
+                pack_halos(n + 1, then[0], then[1])
+                send_halos(n + 1)
         e, h, p = sets[STEPS % 2]
         h_out = pltpu.make_async_copy(h.at[:, 1:7, 8:32, :], out.at[0, 3:6], lsem.at[1])
         p_out = pltpu.make_async_copy(p, out.at[0, 6:9], lsem.at[2])
@@ -383,12 +390,10 @@
         def inside_x(x):
             return jnp.where((x < 3) | two, 1, 0).astype(jnp.int32)
 
-        each(1, lambda m: pos_copy(m).start())
         tabs = tables(permit, conduct, relax, debye, 1.0 / 3.0, 0.25)
         spread = [3 * lanes + r for r in range(3)]
-        packed = [(lanes + 128 * v) for v in range(3)]
-        third = [q // 3 for q in packed]
-        phase = [q - 3 * t for q, t in zip(packed, third)]
+        phase = lanes % 3
+        source = [(128 * ((phase + 3 - r) % 3) + lanes) // 3 for r in range(3)]
 
         def gather_in(ref, lead, ry):
             parts = [ref[(v,) + lead + (pl.ds(ry, 8, stride=3), slice(None))] for v in range(3)]
@@ -417,6 +422,8 @@
             return carry
 
         lax.fori_loop(0, 6, fine_factors, 0)
+        all_here()
+        each(1, lambda m: pos_copy(m).start())
         for cp in f_in:
             cp.wait()
         for c in range(3):
@@ -597,7 +604,7 @@
             def substep(s, carry):
                 weight = (s + 1).astype(F32) * (1.0 / 3.0)
                 drv[...] = ear[0] + weight * (ear[1] - ear[0])
-                return lax.fori_loop(0, 6, at_layer, carry)
+                return lax.fori_loop(0, 6, at_layer, carry, unroll=True)
 
             lax.fori_loop(0, 3, substep, 0)
             for i in range(2):
@@ -635,9 +642,10 @@
                     parts = [ff[c, x + lift, 3 * ry + r] for r in range(3)]
                     if c >= 6:
                         parts = [part * fk[4, x, 3 * ry + r] for r, part in enumerate(parts)]
+                    got = [pick(part, source[r]) for r, part in enumerate(parts)]
                     for v in range(3):
-                        got = [pick(part, third[v]) for part in parts]
-                        value = jnp.where(phase[v] == 0, got[0], jnp.where(phase[v] == 1, got[1], got[2]))
+                        a, b, d = (got[(q + 2 * v) % 3] for q in range(3))
+                        value = jnp.where(phase == 0, a, jnp.where(phase == 1, b, d))
                         if lift:
                             value = 0.5 * value
                         stage[v, c, x, pl.ds(ry, 8, stride=3), :] = value

time: 45.1 us -> 40.8 us (0.905)
  Pallas kernels: 41.8 us -> 37.3 us
    pallas_call x1, Pallas kernels: 41.8 us -> 37.3 us  [body(): pl.pallas_call(functools.partial(kernel, nx, ny), out_shape=jax.ShapeDtyp...]
where the time goes in v3:
time: 40.8 us; the launch traced here: 40.3 us
  Pallas kernels  37.3 us (91%)
  local copies, waits for them, and re-layouts  2.96 us (7%)
    pallas_call x1, Pallas kernels, body(): pl.pallas_call(functools.partial(kernel, nx, ny), out_shape=jax.ShapeDtyp...  37.3 us
    unnamed x1, local copies, waits for them, and re-layouts  2.96 us

profile of v3, /device:TPU:40, one launch (start us, length us, event | category | flops | bytes accessed | tf_op | source)
XLA Modules:
  0.0 40.3 jit_solution(16252510010958482601)
XLA Ops:
  0.0 37.3 %shard_map.73 = f32[1,9,6,24,384]{4,3,2,1,0:T(8,128)} custom-call(f32[1,9,6,24,384]{4,3,2,1,0:T(8,128)} %fields.1, s32[1,6,24,384]{3,2,1,0:T(8,128)} %material.1, f32[8]{0:T(128)} %permit.1, f32[8]{0:T(128)} %conduct.1, f32[8]{0:T(128)} %relax.1, f32[8]{0:T(128)} %debye.1, s32[1,1,6]{2,1,0:T(1,128)} %subgrids.1), custom_call_target="tpu_custom_call" | custom-call | tf_op jit(solution)/shard_map/pallas_call | solution.py:681
  37.3 3.0 %copy.9 = f32[1,9,6,24,384]{4,3,2,1,0:T(8,128)} copy(f32[1,9,6,24,384]{4,3,2,1,0:T(8,128)} %shard_map.73) | data formatting | bytes 3981312

commit v4 on v3

--- a/solution.py
+++ b/solution.py
@@ -13,6 +13,8 @@
 
 TO_NEXT = ((-1, 0), (0, -1), (1, 0), (0, 1), (1, -1), (-1, 1))
 XE, YE, XG, YG, C1, C2 = range(6)
+AROUND = TO_NEXT + ((1, 1), (-1, -1))
+SETS = STEPS + 1
 
 
 def lane_iota():
@@ -68,12 +70,13 @@
 def kernel(
     nx, ny,
     fields, material, permit, conduct, relax, debye, subgrids, out,
-    e2, h2, p2, k, stage, mat, ff, fk, pk, pln, own, dl, pd, ear, drv, fkr,
+    e2, h2, p2, k, stage, mat, ff, fk, pk, pln, own, dl, pd, ear, drv, fkr, mext, ew, hw, kw,
     xe_s, ye_s, xg_s, yg_s, c1_s, c2_s,
     xe_r, ye_r, xg_r, yg_r, c1_r, c2_r,
     lat_s, lat_r, ini_s, ini_r, del_s, del_r,
     nx_s, ny_s, nd_s, nx_r, ny_r, nd_r, pos_s, pos_r, place_of,
-    lsem, hs, hr, bs, br, ds, dr, ns, nr, ps, pr,
+    fy_s, fx_r, fy_r, my_s, mx_r, my_r, wm_s, wm_r,
+    lsem, hs, hr, bs, br, ds, dr, ns, nr, ps, pr, fs, fr, ms, mr, ws, wr,
 ):
     grid = lax.axis_index("grid")
     ga = lax.axis_index("gx")
@@ -113,18 +116,18 @@
 
     for cp in m_in:
         cp.start()
-    for ref in (nx_r, ny_r, nd_r, pos_r):
+    for ref in (nx_r, ny_r, nd_r, pos_r, fx_r, fy_r):
         ref[...] = jnp.zeros_like(ref)
 
     @pl.when(coarse)
     def _():
-        for ref in (ye_s, yg_s, pk, pln, own) + recvs:
+        for ref in (ye_s, yg_s, pk, pln, own, mx_r, my_r, my_s, mext) + recvs:
             ref[...] = jnp.zeros_like(ref)
 
     barrier = pltpu.get_barrier_semaphore()
     pl.semaphore_signal(barrier, inc=1, device_id=partner, device_id_type=MESH)
     count = jnp.int32(1)
-    for dx, dy in TO_NEXT:
+    for dx, dy in AROUND:
         count = count + exists(dx, dy).astype(jnp.int32)
 
         @pl.when(exists(dx, dy))
@@ -152,20 +155,39 @@
     def del_copy(n):
         return remote(del_s.at[n], del_r.at[n], ds.at[n], dr.at[n], partner)
 
-    def near_copy(g, m, n):
-        return remote(delta_s[m].at[n], delta_r[m].at[n], ns.at[g, m, n], nr.at[m, n], device(g, *TO_NEXT[m]))
+    def near_copy(m, n):
+        return remote(delta_s[m].at[n], delta_r[m].at[n], ns.at[m, n], nr.at[m, n], device(0, *TO_NEXT[m]))
+
+    def box_copy(m, n):
+        dx, dy = AROUND[m]
+        if dy == 0:
+            src, dst = del_s.at[n], fx_r.at[m // 2, n]
+        else:
+            src, dst = fy_s.at[0 if dy < 0 else 1, n], fy_r.at[m, n]
+        return remote(src, dst, fs.at[m, n], fr.at[m, n], device(1, dx, dy))
 
     def pos_copy(m):
-        return remote(pos_s, pos_r.at[m], ps.at[m], pr.at[m], device(grid, *TO_NEXT[m]))
-
-    def each(turn, fun):
-        for m, (dx, dy) in enumerate(TO_NEXT):
+        return remote(pos_s, pos_r.at[m], ps.at[m], pr.at[m], device(grid, *AROUND[m]))
+
+    def mat_copy(m):
+        dx, dy = TO_NEXT[m]
+        if dy == 0:
+            src, dst = mat.at[:, 0 if dx < 0 else 5], mx_r.at[m // 2]
+        else:
+            src, dst = my_s.at[m], my_r.at[m]
+        return remote(src, dst, ms.at[m], mr.at[m], device(0, dx, dy))
+
+    def win_copy():
+        return remote(wm_s, wm_r, ws.at[0], wr.at[0], partner)
+
+    def each(turn, fun, over=TO_NEXT):
+        for m, (dx, dy) in enumerate(over):
             @pl.when(exists(turn * dx, turn * dy))
             def _():
                 fun(m)
 
     def learn_places():
-        each(-1, lambda m: pos_copy(m).wait_recv())
+        each(-1, lambda m: pos_copy(m).wait_recv(), AROUND)
         cp = pltpu.make_async_copy(pos_r, place_of, lsem.at[6])
         cp.start()
         cp.wait()
@@ -253,9 +275,8 @@
                 h[0, x + 1, 7:8, :] = pln[0, x:x + 1, :]
                 h[2, x + 1, 7:8, :] = pln[1, x:x + 1, :]
 
-        def mend_halos(n):
-            d = n - 1
-            each(-1, lambda m: near_copy(0, m, d).wait_recv())
+        def mend_halos(n, d):
+            each(-1, lambda m: near_copy(m, d).wait_recv())
             for u in range(3):
                 for v in range(3):
                     spot = tile_at(u, v)
@@ -315,15 +336,48 @@
 
             lax.fori_loop(0, 6, at_x, 0, unroll=True)
 
-        sets = [(e2.at[q], h2.at[q], p2.at[q]) for q in range(2)]
+        def material_window():
+            each(-1, lambda m: mat_copy(m).wait_recv())
+            for v in range(3):
+                mext[v, 1:7, 8:32, :] = mat[v]
+                mext[v, 7, 8:32, :] = mx_r[0, v]
+                mext[v, 0, 8:32, :] = mx_r[1, v]
+                for x in range(6):
+                    mext[v, x + 1, 32:33, :] = my_r[YE, v, x:x + 1, :]
+                    mext[v, x + 1, 7:8, :] = my_r[YG, v, x:x + 1, :]
+                mext[v, 0, 32:33, :] = my_r[C1, v, 0:1, :]
+                mext[v, 7, 7:8, :] = my_r[C2, v, 0:1, :]
+            for u2 in range(2):
+                for v2 in range(2):
+                    found = [jnp.zeros((8, 128), jnp.int32)] * 4
+                    for u in range(-1, 4):
+                        for v in range(3):
+                            if u % 2 != u2 or v % 2 != v2:
+                                continue
+                            ok = (rows + 8 * u >= y0 - 1) & (rows + 8 * u < y0 + 9)
+                            ok = ok & (lanes + 128 * v >= z0 - 1) & (lanes + 128 * v < z0 + 129)
+                            for xr in range(4):
+                                found[xr] = jnp.where(ok, mext[v, x0 + xr, 8 * u + 8:8 * u + 16, :], found[xr])
+                    for xr in range(4):
+                        wm_s[xr, u2, v2] = found[xr]
+            win_copy().start()
+
+        sets = [(e2.at[q], h2.at[q], p2.at[q]) for q in range(3)]
         e_in.wait()
         h_in.wait()
         pack_halos(0, sets[0][0], sets[0][1])
         all_here()
         send_halos(0)
-        each(1, lambda m: pos_copy(m).start())
+        each(1, lambda m: pos_copy(m).start(), AROUND)
         for cp in m_in:
             cp.wait()
+        for v in range(3):
+            for x in range(6):
+                my_s[YE, v, x:x + 1, :] = mat[v, x, 0:1, :]
+                my_s[YG, v, x:x + 1, :] = mat[v, x, 23:24, :]
+            my_s[C1, v] = jnp.broadcast_to(mat[v, 5, 0:1, :], (8, 128))
+            my_s[C2, v] = jnp.broadcast_to(mat[v, 0, 23:24, :], (8, 128))
+        each(1, lambda m: mat_copy(m).start())
         tabs = tables(permit, conduct, relax, debye, 1.0, 0.5)
 
         def factors(x, carry):
@@ -338,31 +392,45 @@
         for i in range(2):
             for c in range(3):
                 ini_s[c, i] = cut(lambda x, r, l: e2[0, c, x, r, l], i)
-            for q in range(2):
-                ini_s[3 + q, i] = cut(lambda x, r, l: k[q, x, r, l], i)
         ini_copy().start()
         p_in.wait()
-        for n in range(STEPS):
-            now, then = sets[n % 2], sets[(n + 1) % 2]
-            each(-1, lambda m: halo_copy(m, n).wait_recv())
-            if n == 0:
-                put_halos(n, now[0], then[1])
-                update(*now, *then)
-                cut_latest(0, then[0])
-                learn_places()
-            else:
-                put_halos(n, now[0], then[1])
-                update(*now, then[0], then[1], None)
-                cut_latest(n, then[0])
-                del_copy(n - 1).wait_recv()
-                place(n - 1, now[0])
-                mend_halos(n)
-                put_halos(n, now[0], then[1])
-                update(*now, *then)
-            if n + 1 < STEPS:
-                pack_halos(n + 1, then[0], then[1])
-                send_halos(n + 1)
-        e, h, p = sets[STEPS % 2]
+
+        def advance(slot, source, target):
+            put_halos(slot, source[0], target[1])
+            update(*source, *target)
+
+        def arrive(slot):
+            each(-1, lambda m: halo_copy(m, slot).wait_recv())
+
+        def leave(slot, state):
+            pack_halos(slot, state[0], state[1])
+            send_halos(slot)
+
+        arrive(0)
+        advance(0, sets[0], sets[1])
+        cut_latest(0, sets[1][0])
+        leave(1, sets[1])
+        learn_places()
+        material_window()
+        arrive(1)
+        advance(1, sets[1], sets[2])
+        cut_latest(1, sets[2][0])
+        leave(2, sets[2])
+        arrive(2)
+        put_halos(2, sets[2][0], sets[0][1])
+        update(*sets[2], sets[0][0], sets[0][1], None)
+        cut_latest(2, sets[0][0])
+        del_copy(0).wait_recv()
+        place(0, sets[1][0])
+        mend_halos(1, 0)
+        advance(1, sets[1], sets[0])
+        leave(3, sets[0])
+        arrive(3)
+        del_copy(1).wait_recv()
+        place(1, sets[0][0])
+        mend_halos(3, 1)
+        advance(3, sets[0], sets[2])
+        e, h, p = sets[2]
         h_out = pltpu.make_async_copy(h.at[:, 1:7, 8:32, :], out.at[0, 3:6], lsem.at[1])
         p_out = pltpu.make_async_copy(p, out.at[0, 6:9], lsem.at[2])
         h_out.start()
@@ -372,9 +440,12 @@
         e_out = pltpu.make_async_copy(e.at[:, 0:6, 0:24, :], out.at[0, 0:3], lsem.at[0])
         e_out.start()
 
-        each(1, lambda m: pos_copy(m).wait_send())
+        each(1, lambda m: pos_copy(m).wait_send(), AROUND)
+        each(1, lambda m: mat_copy(m).wait_send())
+        win_copy().wait_send()
+        for n in range(SETS):
+            each(1, lambda m: halo_copy(m, n).wait_send())
         for n in range(STEPS):
-            each(1, lambda m: halo_copy(m, n).wait_send())
             lat_copy(n).wait_send()
         ini_copy().wait_send()
         h_out.wait()
@@ -383,6 +454,8 @@
 
     @pl.when(jnp.logical_not(coarse))
     def _():
+        for ref in (ny_s, fy_s):
+            ref[...] = jnp.zeros_like(ref)
         none = jnp.zeros((8, 128), jnp.int32)
         inside = (rows < ly) & (lanes < lz)
         two = lx == 2
@@ -423,7 +496,7 @@
 
         lax.fori_loop(0, 6, fine_factors, 0)
         all_here()
-        each(1, lambda m: pos_copy(m).start())
+        each(1, lambda m: pos_copy(m).start(), AROUND)
         for cp in f_in:
             cp.wait()
         for c in range(3):
@@ -528,63 +601,111 @@
         def as_int(flag):
             return jnp.where(flag, 1, 0).astype(jnp.int32)
 
-        def correction(n):
-            each(-1, lambda m: near_copy(1, m, n - 1).wait_recv())
-            d = n - 1
-            region = w_in(at_y, y0, 8) & w_in(at_z, z0, 128)
-            wide_none = jnp.zeros((16, 256), jnp.int32)
+        def up_y(a):
+            return pltpu.roll(a, 15, 0)
+
+        def up_z(a):
+            return pltpu.roll(a, 255, 1)
+
+        def down_y(a):
+            return pltpu.roll(a, 1, 0)
+
+        def down_z(a):
+            return pltpu.roll(a, 1, 1)
+
+        region = w_in(at_y, y0, 8) & w_in(at_z, z0, 128)
+        w_none = jnp.zeros((16, 256), jnp.int32)
+        global_y = at_y + 24 * gb
+        held_yz = (at_z >= 0) & (global_y >= 0)
+        in_yz = held_yz & (at_z < 384) & (global_y < 24 * ny)
+
+        def changes(d, reach):
             w = {}
             for c in range(3):
-                for xr in range(-1, 3):
+                for xr in range(-reach, 2 + reach):
                     w[c, xr] = jnp.where(region, twice(del_s[d, c, xr]), 0.0) if 0 <= xr < 2 else jnp.zeros((16, 256), F32)
-            for m, xr, at_edge in ((XE, 2, x0 == 4), (XG, -1, x0 == 0)):
-                ok = w_in(at_y, place_of[m, 1, 0], 8) & w_in(at_z, place_of[m, 2, 0], 128)
-                ok = ok & (as_int(at_edge) + wide_none > 0)
-                for c in range(3):
-                    w[c, xr] = w[c, xr] + jnp.where(ok, twice(nx_r[m // 2, d, c]), 0.0)
-            for m, y in ((YE, 24), (YG, -1)):
-                ok = (at_y == y) & w_in(at_z, place_of[m, 2, 0], 128)
-                for c in range(3):
-                    two_rows = [ny_r[m // 2, d, 2 * c + i:2 * c + i + 1, :] for i in range(2)]
+            for m, (dx, dy) in enumerate(AROUND):
+                far_x, far_y, far_z = place_of[m, 0, 0], place_of[m, 1, 0], place_of[m, 2, 0]
+                ok = w_in(at_z, far_z, 128)
+                if dy == 0:
+                    ok = ok & w_in(at_y, far_y, 8)
+                else:
+                    ok = ok & w_in(at_y, 24 if dy < 0 else -2, 2)
+                for xr in {0: range(-reach, 2 + reach), -1: range(2, 2 + reach), 1: range(-reach, 0)}[dx]:
+                    i = x0 + xr + 6 * dx - far_x
+                    s0 = jnp.where(i == 0, 1.0, 0.0).astype(F32)
+                    s1 = jnp.where(i == 1, 1.0, 0.0).astype(F32)
+                    for c in range(3):
+                        if dy == 0:
+                            tile = s0 * fx_r[m // 2, d, c, 0] + s1 * fx_r[m // 2, d, c, 1]
+                        else:
+                            pair = [s0 * fy_r[m, d, 6 * r + 2 * c:6 * r + 2 * c + 1, :]
+                                    + s1 * fy_r[m, d, 6 * r + 2 * c + 1:6 * r + 2 * c + 2, :] for r in range(2)]
+                            low = 0 if dy < 0 else 6
+                            tile = jnp.where(rows == low, jnp.broadcast_to(pair[0], (8, 128)),
+                                             jnp.broadcast_to(pair[1], (8, 128)))
+                        w[c, xr] = w[c, xr] + jnp.where(ok, twice(tile), 0.0)
+            return w
+
+        def turned_ahead(w, xr):
+            ex, ey, ez = (w[c, xr] for c in range(3))
+            moved = ((up_y(ez) - ez) - (up_z(ey) - ey), (up_z(ex) - ex) - (w[2, xr + 1] - ez),
+                     (w[1, xr + 1] - ey) - (up_y(ex) - ex))
+            ok = held_yz & (as_int(x0 + xr + 6 * ga >= 0) + w_none > 0)
+            return [jnp.where(ok, -0.5 * part, 0.0) for part in moved]
+
+        def turned_behind(hh, xr):
+            hx, hy, hz = (hh[c, xr] for c in range(3))
+            return ((hz - down_y(hz)) - (hy - down_z(hy)), (hx - down_z(hx)) - (hz - hh[2, xr - 1]),
+                    (hy - hh[1, xr - 1]) - (hx - down_y(hx)))
+
+        def on_region(wide):
+            kept = jnp.where(region, wide, 0.0)
+            return (kept[0:8, 0:128] + kept[0:8, 128:256]) + (kept[8:16, 0:128] + kept[8:16, 128:256])
+
+        def window_factors():
+            win_copy().wait_recv()
+            slab = tables(permit, conduct, relax, debye, 1.0, 0.5)
+            for xr in range(4):
+                for u2 in range(2):
+                    for v2 in range(2):
+                        here = wm_r[xr, u2, v2]
+                        spot = (xr, slice(8 * u2, 8 * u2 + 8), slice(128 * v2, 128 * v2 + 128))
+                        for q in range(2):
+                            kw[(q,) + spot] = pick(slab[q], here)
+                        kw[(2,) + spot] = pick(slab[2], here) * pick(slab[4], here)
+
+        def respond(n):
+            each(-1, lambda m: box_copy(m, n - 1).wait_recv(), AROUND)
+            hh = {}
+            if n == 1:
+                w = changes(0, 2)
+                for xr in range(-2, 3):
+                    for c, part in enumerate(turned_ahead(w, xr)):
+                        hh[c, xr] = part
+                        if -1 <= xr <= 1:
+                            hw[c, xr + 1] = part
+                layers = range(-1, 3)
+            else:
+                w = changes(1, 1)
+                for c in range(3):
                     for xr in range(-1, 3):
-                        i = x0 + xr - place_of[m, 0, 0]
-                        s0 = jnp.where(i == 0, 1.0, 0.0).astype(F32)
-                        s1 = jnp.where(i == 1, 1.0, 0.0).astype(F32)
-                        row = jnp.broadcast_to(s0 * two_rows[0] + s1 * two_rows[1], (8, 128))
-                        w[c, xr] = w[c, xr] + jnp.where(ok, twice(row), 0.0)
-            for m, c, xr, y, at_edge in ((C1, 0, -1, 24, x0 == 0), (C2, 1, 2, -1, x0 == 4)):
-                ok = (at_y == y) & w_in(at_z, place_of[m, 2, 0], 128) & (as_int(at_edge) + wide_none > 0)
-                w[c, xr] = w[c, xr] + jnp.where(ok, twice(nd_r[m - 4, d]), 0.0)
-
-            def up_y(a):
-                return pltpu.roll(a, 15, 0)
-
-            def up_z(a):
-                return pltpu.roll(a, 255, 1)
-
-            def down_y(a):
-                return pltpu.roll(a, 1, 0)
-
-            def down_z(a):
-                return pltpu.roll(a, 1, 1)
-
-            held = (at_z >= 0) & (at_y + 24 * gb >= 0)
-            hh = {}
-            for xr in range(-1, 2):
-                ok = held & (as_int(x0 + xr + 6 * ga >= 0) + wide_none > 0)
-                ex, ey, ez = (w[c, xr] for c in range(3))
-                moved = ((up_y(ez) - ez) - (up_z(ey) - ey), (up_z(ex) - ex) - (w[2, xr + 1] - ez),
-                         (w[1, xr + 1] - ey) - (up_y(ex) - ex))
-                for c in range(3):
-                    hh[c, xr] = jnp.where(ok, -0.5 * moved[c], 0.0)
-            for xr in range(2):
-                hx, hy, hz = (hh[c, xr] for c in range(3))
-                curls = ((hz - down_y(hz)) - (hy - down_z(hy)), (hx - down_z(hx)) - (hz - hh[2, xr - 1]),
-                         (hy - hh[1, xr - 1]) - (hx - down_y(hx)))
-                for c in range(3):
-                    kept = jnp.where(region, curls[c], 0.0)
-                    tile = (kept[0:8, 0:128] + kept[0:8, 128:256]) + (kept[8:16, 0:128] + kept[8:16, 128:256])
-                    ear[1, c, xr] = to_box(lat_r[n, c, xr] + ini_r[3, xr] * del_s[d, c, xr] + ini_r[4, xr] * tile)
+                        w[c, xr] = w[c, xr] + ew[c, xr + 1]
+                for xr in range(-1, 2):
+                    for c, part in enumerate(turned_ahead(w, xr)):
+                        hh[c, xr] = hw[c, xr + 1] + part
+                layers = range(2)
+            for xr in layers:
+                ok = in_yz & (as_int((x0 + xr + 6 * ga >= 0) & (x0 + xr + 6 * ga < 6 * nx)) + w_none > 0)
+                for c, curl in enumerate(turned_behind(hh, xr)):
+                    value = kw[0, xr + 1] * w[c, xr] + kw[1, xr + 1] * curl
+                    if n == 1:
+                        value = jnp.where(ok, value, 0.0)
+                        ew[c, xr + 1] = value
+                    else:
+                        value = value + kw[2, xr + 1] * ew[c, xr + 1]
+                    if 0 <= xr < 2:
+                        ear[1, c, xr] = to_box(lat_r[n, c, xr] + on_region(value))
 
         learn_places()
         ini_copy().wait_recv()
@@ -599,7 +720,9 @@
                     for i in range(2):
                         ear[1, c, i] = to_box(lat_r[0, c, i])
             else:
-                correction(n)
+                if n == 1:
+                    window_factors()
+                respond(n)
 
             def substep(s, carry):
                 weight = (s + 1).astype(F32) * (1.0 / 3.0)
@@ -617,6 +740,20 @@
                     ear[0, c, i] = latest + delta
                     del_s[n, c, i] = from_box(delta)
             if n + 1 < STEPS:
+                for r in range(2):
+                    low = jnp.where(y0 <= r, 1.0, 0.0).astype(F32)
+                    high = jnp.where(y0 >= 15 + r, 1.0, 0.0).astype(F32)
+                    for c in range(3):
+                        for i in range(2):
+                            row = 6 * r + 2 * c + i
+                            fy_s[0, n, row:row + 1, :] = low * del_s[n, c, i, r:r + 1, :]
+                            fy_s[1, n, row:row + 1, :] = high * del_s[n, c, i, 6 + r:7 + r, :]
+                for m in (4, 5, 6, 7, 0, 2, 1, 3):
+                    dx, dy = AROUND[m]
+
+                    @pl.when(exists(dx, dy))
+                    def _():
+                        box_copy(m, n).start()
                 low, high = (jnp.where(x0 == q, 1.0, 0.0).astype(F32) for q in (0, 4))
                 left, right = (jnp.where(y0 == q, 1.0, 0.0).astype(F32) for q in (0, 16))
                 for c in range(3):
@@ -625,13 +762,10 @@
                     for i in range(2):
                         ny_s[0, n, 2 * c + i:2 * c + i + 1, :] = left * del_s[n, c, i, 0:1, :]
                         ny_s[1, n, 2 * c + i:2 * c + i + 1, :] = right * del_s[n, c, i, 7:8, :]
-                for q in range(2):
-                    ny_s[q, n, 6:8, :] = jnp.zeros((2, 128), F32)
                 nd_s[0, n] = jnp.broadcast_to((high * left) * del_s[n, 0, 1, 0:1, :], (8, 128))
                 nd_s[1, n] = jnp.broadcast_to((low * right) * del_s[n, 1, 0, 7:8, :], (8, 128))
-                each(1, lambda m: near_copy(1, m, n).start())
                 del_copy(n).start()
-                each(1, lambda m: near_copy(0, m, n).start())
+                each(1, lambda m: near_copy(m, n).start())
             else:
                 del_copy(n).start()
 
@@ -655,12 +789,12 @@
         f_out = [pltpu.make_async_copy(stage.at[v], out.at[0, :, :, :, pl.ds(128 * v, 128)], lsem.at[v]) for v in range(3)]
         for cp in f_out:
             cp.start()
-        each(1, lambda m: pos_copy(m).wait_send())
+        each(1, lambda m: pos_copy(m).wait_send(), AROUND)
         for n in range(STEPS):
             del_copy(n).wait_send()
             if n + 1 < STEPS:
-                for g in range(2):
-                    each(1, lambda m: near_copy(g, m, n).wait_send())
+                each(1, lambda m: near_copy(m, n).wait_send())
+                each(1, lambda m: box_copy(m, n).wait_send(), AROUND)
         for cp in f_out:
             cp.wait()
 
@@ -672,9 +806,9 @@
         vm = pltpu.VMEM
         dma = pltpu.SemaphoreType.DMA
         slots = [
-            vm((STEPS, 2, 24, 384), F32), vm((STEPS, 2, 8, 384), F32),
-            vm((STEPS, 2, 24, 384), F32), vm((STEPS, 2, 8, 384), F32),
-            vm((STEPS, 8, 384), F32), vm((STEPS, 8, 384), F32),
+            vm((SETS, 2, 24, 384), F32), vm((SETS, 2, 8, 384), F32),
+            vm((SETS, 2, 24, 384), F32), vm((SETS, 2, 8, 384), F32),
+            vm((SETS, 8, 384), F32), vm((SETS, 8, 384), F32),
         ]
         region = (3, 2, 8, 128)
         near = [vm((2, STEPS - 1, 3, 8, 128), F32), vm((2, STEPS - 1, 8, 128), F32), vm((2, STEPS - 1, 8, 128), F32)]
@@ -684,18 +818,23 @@
             in_specs=[pl.BlockSpec(memory_space=pl.ANY)] * 2 + [pl.BlockSpec(memory_space=pltpu.SMEM)] * 5,
             out_specs=pl.BlockSpec(memory_space=pl.ANY),
             scratch_shapes=[
-                vm((2, 3, 7, 32, 384), F32), vm((2, 3, 7, 32, 384), F32), vm((2, 3, 6, 24, 384), F32), vm((5, 6, 24, 384), F32),
+                vm((3, 3, 7, 32, 384), F32), vm((3, 3, 7, 32, 384), F32), vm((3, 3, 6, 24, 384), F32), vm((5, 6, 24, 384), F32),
                 vm((3, 9, 6, 24, 128), F32), vm((3, 6, 24, 128), jnp.int32),
                 vm((9, 7, 9, 8, 128), F32), vm((5, 6, 9, 8, 128), F32),
                 vm((5, 16, 384), F32), vm((2, 8, 384), F32), vm((2, 8, 384), F32), vm((3, 32, 384), F32), vm((3, 8, 384), F32),
                 vm((2,) + region, F32), vm(region, F32), vm((6, 9, 8, 128), F32),
+                vm((3, 8, 40, 128), jnp.int32), vm((3, 4, 16, 256), F32), vm((3, 3, 16, 256), F32), vm((3, 4, 16, 256), F32),
                 *slots, *slots,
-                vm((STEPS,) + region, F32), vm((STEPS,) + region, F32), vm((5, 2, 8, 128), F32), vm((5, 2, 8, 128), F32),
+                vm((STEPS,) + region, F32), vm((STEPS,) + region, F32), vm(region, F32), vm(region, F32),
                 vm((STEPS,) + region, F32), vm((STEPS,) + region, F32),
-                *near, *near, vm((8, 128), jnp.int32), vm((6, 8, 128), jnp.int32), pltpu.SMEM((6, 8, 128), jnp.int32),
-                dma((7,)), dma((6, STEPS)), dma((6, STEPS)),
+                *near, *near, vm((8, 128), jnp.int32), vm((8, 8, 128), jnp.int32), pltpu.SMEM((8, 8, 128), jnp.int32),
+                vm((2, STEPS - 1, 16, 128), F32), vm((2, STEPS - 1) + region, F32), vm((8, STEPS - 1, 16, 128), F32),
+                vm((6, 3, 8, 128), jnp.int32), vm((2, 3, 24, 128), jnp.int32), vm((6, 3, 8, 128), jnp.int32),
+                vm((4, 2, 2, 8, 128), jnp.int32), vm((4, 2, 2, 8, 128), jnp.int32),
+                dma((7,)), dma((6, SETS)), dma((6, SETS)),
                 dma((STEPS + 1,)), dma((STEPS + 1,)), dma((STEPS,)), dma((STEPS,)),
-                dma((2, 6, STEPS)), dma((6, STEPS)), dma((6,)), dma((6,)),
+                dma((6, STEPS)), dma((6, STEPS)), dma((8,)), dma((8,)),
+                dma((8, STEPS)), dma((8, STEPS)), dma((6,)), dma((6,)), dma((1,)), dma((1,)),
             ],
             compiler_params=pltpu.CompilerParams(
                 collective_id=0, has_side_effects=True, vmem_limit_bytes=63 * 1024 * 1024),

time: 40.8 us -> 37.1 us (0.909)
  Pallas kernels: 37.3 us -> 33.9 us
    pallas_call x1, Pallas kernels: 37.3 us -> 33.9 us  [body(): pl.pallas_call(functools.partial(kernel, nx, ny), out_shape=jax.ShapeDtyp...]
where the time goes in v4:
time: 37.1 us; the launch traced here: 36.8 us
  Pallas kernels  33.9 us (91%)
  local copies, waits for them, and re-layouts  2.96 us (8%)
    pallas_call x1, Pallas kernels, body(): pl.pallas_call(functools.partial(kernel, nx, ny), out_shape=jax.ShapeDtyp...  33.9 us
    unnamed x1, local copies, waits for them, and re-layouts  2.96 us

profile of v4, /device:TPU:40, one launch (start us, length us, event | category | flops | bytes accessed | tf_op | source)
XLA Modules:
  0.0 36.8 jit_solution(4422851940823386110)
XLA Ops:
  0.0 33.9 %shard_map.73 = f32[1,9,6,24,384]{4,3,2,1,0:T(8,128)} custom-call(f32[1,9,6,24,384]{4,3,2,1,0:T(8,128)} %fields.1, s32[1,6,24,384]{3,2,1,0:T(8,128)} %material.1, f32[8]{0:T(128)} %permit.1, f32[8]{0:T(128)} %conduct.1, f32[8]{0:T(128)} %relax.1, f32[8]{0:T(128)} %debye.1, s32[1,1,6]{2,1,0:T(1,128)} %subgrids.1), custom_call_target="tpu_custom_call" | custom-call | tf_op jit(solution)/shard_map/pallas_call | solution.py:815
  33.9 3.0 %copy.9 = f32[1,9,6,24,384]{4,3,2,1,0:T(8,128)} copy(f32[1,9,6,24,384]{4,3,2,1,0:T(8,128)} %shard_map.73) | data formatting | bytes 3981312

commit v5 on v4

--- a/solution.py
+++ b/solution.py
@@ -69,8 +69,8 @@
 
 def kernel(
     nx, ny,
-    fields, material, permit, conduct, relax, debye, subgrids, out,
-    e2, h2, p2, k, stage, mat, ff, fk, pk, pln, own, dl, pd, ear, drv, fkr, mext, ew, hw, kw,
+    fields, material, permit_in, conduct_in, relax_in, debye_in, subgrids_in, out,
+    permit, conduct, relax, debye, subgrids, e2, h2, p2, k, stage, mat, ff, fk, pk, pln, own, dl, pd, ear, drv, fkr, mext, ew, hw, kw,
     xe_s, ye_s, xg_s, yg_s, c1_s, c2_s,
     xe_r, ye_r, xg_r, yg_r, c1_r, c2_r,
     lat_s, lat_r, ini_s, ini_r, del_s, del_r,
@@ -82,8 +82,6 @@
     ga = lax.axis_index("gx")
     gb = lax.axis_index("gy")
     coarse = grid == 0
-    x0, y0, z0 = subgrids[0, 0, 0], subgrids[0, 0, 1], subgrids[0, 0, 2]
-    lx, ly, lz = subgrids[0, 0, 3], subgrids[0, 0, 4], subgrids[0, 0, 5]
     sends = (xe_s, ye_s, xg_s, yg_s, c1_s, c2_s)
     recvs = (xe_r, ye_r, xg_r, yg_r, c1_r, c2_r)
     delta_s = (nx_s.at[0], ny_s.at[0], nx_s.at[1], ny_s.at[1], nd_s.at[0], nd_s.at[1])
@@ -116,12 +114,18 @@
 
     for cp in m_in:
         cp.start()
+    scalars = [
+        pltpu.make_async_copy(a, b, lsem.at[7 + q])
+        for q, (a, b) in enumerate(((permit_in, permit), (conduct_in, conduct), (relax_in, relax), (debye_in, debye),
+                                    (subgrids_in, subgrids)))]
+    for cp in scalars:
+        cp.start()
     for ref in (nx_r, ny_r, nd_r, pos_r, fx_r, fy_r):
         ref[...] = jnp.zeros_like(ref)
 
     @pl.when(coarse)
     def _():
-        for ref in (ye_s, yg_s, pk, pln, own, mx_r, my_r, my_s, mext) + recvs:
+        for ref in (mx_r, my_r) + recvs:
             ref[...] = jnp.zeros_like(ref)
 
     barrier = pltpu.get_barrier_semaphore()
@@ -134,6 +138,15 @@
         def _():
             pl.semaphore_signal(barrier, inc=1, device_id=(grid, ga + dx, gb + dy), device_id_type=MESH)
 
+    @pl.when(coarse)
+    def _():
+        for ref in (ye_s, yg_s, pk, pln, own, my_s, mext):
+            ref[...] = jnp.zeros_like(ref)
+
+    for cp in scalars:
+        cp.wait()
+    x0, y0, z0 = subgrids[0, 0, 0], subgrids[0, 0, 1], subgrids[0, 0, 2]
+    lx, ly, lz = subgrids[0, 0, 3], subgrids[0, 0, 4], subgrids[0, 0, 5]
     pos_s[...] = jnp.where(rows == 0, x0, jnp.where(rows == 1, y0, z0))
 
     def all_here():
@@ -144,6 +157,8 @@
             src_ref=src, dst_ref=dst, send_sem=send, recv_sem=recv, device_id=target, device_id_type=MESH)
 
     def halo_copy(m, n):
+        if m in (C1, C2):
+            return remote(sends[m].at[n, 0:1], recvs[m].at[n, 0:1], hs.at[m, n], hr.at[m, n], device(grid, *TO_NEXT[m]))
         return remote(sends[m].at[n], recvs[m].at[n], hs.at[m, n], hr.at[m, n], device(grid, *TO_NEXT[m]))
 
     def lat_copy(n):
@@ -223,8 +238,8 @@
                     lat_s[n, c, i] = cut(lambda x, r, l: e[c, x, r, l], i)
             lat_copy(n).start()
 
-        def place(n, e):
-            def at_x(x, carry):
+        def place(n, e, done=None):
+            for x in range(6):
                 s0 = jnp.where(x == x0, 1.0, 0.0).astype(F32)
                 s1 = jnp.where(x == x0 + 1, 1.0, 0.0).astype(F32)
                 for c in range(3):
@@ -233,31 +248,43 @@
                         for v in range(3):
                             spot = (c, x) + tile_at(u, v)
                             e[spot] = e[spot] + jnp.where(row_ok[u] & lane_ok[v], tile, 0.0)
-                return carry
-
-            lax.fori_loop(0, 6, at_x, 0)
-
-        def pack_halos(n, e, h):
-            for x in range(6):
-                ye_s[n, 0, x:x + 1, :] = e[0, x, 0:1, :]
-                ye_s[n, 1, x:x + 1, :] = e[2, x, 0:1, :]
-                for c in range(3):
-                    pk[c, x:x + 1, :] = e[c, x, 23:24, :]
-                pk[3, x:x + 1, :] = h[0, x + 1, 31:32, :]
-                pk[4, x:x + 1, :] = h[2, x + 1, 31:32, :]
-            xe_s[n] = e[1:3, 0, 0:24, :]
+                if done is not None:
+                    done[x].start()
+
+        def send_halo(m, n):
+            @pl.when(exists(*TO_NEXT[m]))
+            def _():
+                halo_copy(m, n).start()
+
+        def leave_high(n, e, h):
+            c1_s[n, 0:1, :] = e[0, 5, 0:1, :]
+            send_halo(C1, n)
             ex, ey, ez = e[0, 5, 0:24, :], e[1, 5, 0:24, :], e[2, 5, 0:24, :]
             exy = jnp.where(wide == 23, 0.0, e[0, 5, 1:25, :])
             xg_s[n, 0] = h[1, 6, 8:32, :] - 0.5 * (zfwd(ex) - ex + ez)
             xg_s[n, 1] = h[2, 6, 8:32, :] + 0.5 * (ey + exy - ex)
+            send_halo(XG, n)
+
+        def leave_low(n, e):
+            c2_s[n, 0:1, :] = e[1, 0, 23:24, :]
+            send_halo(C2, n)
+            xe_s[n] = e[1:3, 0, 0:24, :]
+            send_halo(XE, n)
+
+        def leave_y(n, e, h):
+            for x in range(6):
+                ye_s[n, 0, x:x + 1, :] = e[0, x, 0:1, :]
+                ye_s[n, 1, x:x + 1, :] = e[2, x, 0:1, :]
+            send_halo(YE, n)
+            for x in range(6):
+                for c in range(3):
+                    pk[c, x:x + 1, :] = e[c, x, 23:24, :]
+                pk[3, x:x + 1, :] = h[0, x + 1, 31:32, :]
+                pk[4, x:x + 1, :] = h[2, x + 1, 31:32, :]
             px, py, pz = pk[0, 0:8, :], pk[1, 0:8, :], pk[2, 0:8, :]
             yg_s[n, 0] = pk[3, 0:8, :] + 0.5 * (pz + zfwd(py) - py)
             yg_s[n, 1] = pk[4, 0:8, :] - 0.5 * (pk[1, 1:9, :] - py + px)
-            c1_s[n] = jnp.broadcast_to(e[0, 5, 0:1, :], (8, 384))
-            c2_s[n] = jnp.broadcast_to(e[1, 0, 23:24, :], (8, 384))
-
-        def send_halos(n):
-            each(1, lambda m: halo_copy(m, n).start())
+            send_halo(YG, n)
 
         def put_halos(n, e, h):
             e[1:3, 6, 0:24, :] = xe_r[n]
@@ -268,7 +295,7 @@
                 own[0, x:x + 1, :] = e[0, x, 0:1, :]
                 own[1, x:x + 1, :] = e[2, x, 0:1, :]
             pln[0] = flag_y * (yg_r[n, 0] - 0.5 * own[1])
-            pln[1] = flag_y * (yg_r[n, 1] + 0.5 * (own[0] - jnp.where(plane == 5, c2_r[n], 0.0)))
+            pln[1] = flag_y * (yg_r[n, 1] + 0.5 * (own[0] - jnp.where(plane == 5, jnp.broadcast_to(c2_r[n, 0:1, :], (8, 384)), 0.0)))
             for x in range(6):
                 e[0, x, 24:25, :] = ye_r[n, 0, x:x + 1, :]
                 e[2, x, 24:25, :] = ye_r[n, 1, x:x + 1, :]
@@ -308,33 +335,51 @@
                     spot = (n, slice(0, 8), slice(128 * v, 128 * v + 128))
                     ref[spot] = ref[spot] + jnp.where(lane_in(place_of[m, 2, 0], v), keep[d], 0.0)
 
-        def update(e, h, p, ed, hd, pd_):
-            def at_x(x, carry):
+        def update(e, h, p, ed, hd, pd_, slot=None, cut_to=None):
+            def magnetic(x):
                 for u in range(3):
                     r = slice(8 * u, 8 * u + 8)
                     ra = slice(8 * u + 1, 8 * u + 9)
                     rh = slice(8 * u + 8, 8 * u + 16)
+                    ex, ey, ez = e[0, x, r, :], e[1, x, r, :], e[2, x, r, :]
+                    hd[0, x + 1, rh, :] = h[0, x + 1, rh, :] - 0.5 * ((e[2, x, ra, :] - ez) - (zfwd(ey) - ey))
+                    hd[1, x + 1, rh, :] = h[1, x + 1, rh, :] - 0.5 * ((zfwd(ex) - ex) - (e[2, x + 1, r, :] - ez))
+                    hd[2, x + 1, rh, :] = h[2, x + 1, rh, :] - 0.5 * ((e[1, x + 1, r, :] - ey) - (e[0, x, ra, :] - ex))
+
+            def electric(x):
+                for u in range(3):
+                    r = slice(8 * u, 8 * u + 8)
+                    rh = slice(8 * u + 8, 8 * u + 16)
                     rb = slice(8 * u + 7, 8 * u + 15)
-                    ex, ey, ez = e[0, x, r, :], e[1, x, r, :], e[2, x, r, :]
-                    hx = h[0, x + 1, rh, :] - 0.5 * ((e[2, x, ra, :] - ez) - (zfwd(ey) - ey))
-                    hy = h[1, x + 1, rh, :] - 0.5 * ((zfwd(ex) - ex) - (e[2, x + 1, r, :] - ez))
-                    hz = h[2, x + 1, rh, :] - 0.5 * ((e[1, x + 1, r, :] - ey) - (e[0, x, ra, :] - ex))
-                    hd[0, x + 1, rh, :] = hx
-                    hd[1, x + 1, rh, :] = hy
-                    hd[2, x + 1, rh, :] = hz
+                    hx, hy, hz = hd[0, x + 1, rh, :], hd[1, x + 1, rh, :], hd[2, x + 1, rh, :]
                     cx = (hz - hd[2, x + 1, rb, :]) - (hy - zbwd(hy))
                     cy = (hx - zbwd(hx)) - (hz - hd[2, x, rh, :])
                     cz = (hy - hd[1, x, rh, :]) - (hx - hd[0, x + 1, rb, :])
                     ka, kc, kb, kf, kg = (k[q, x, r, :] for q in range(5))
-                    for c, (old, curl) in enumerate(((ex, cx), (ey, cy), (ez, cz))):
+                    for c, curl in enumerate((cx, cy, cz)):
                         pol = p[c, x, r, :]
-                        new = ka * old + kc * curl + kb * pol
+                        new = ka * e[c, x, r, :] + kc * curl + kb * pol
                         ed[c, x, r, :] = new
                         if pd_ is not None:
                             pd_[c, x, r, :] = kf * pol + kg * new
-                return carry
-
-            lax.fori_loop(0, 6, at_x, 0, unroll=True)
+
+            magnetic(4)
+            magnetic(5)
+            electric(5)
+            if slot is not None:
+                leave_high(slot, ed, hd)
+            magnetic(0)
+            electric(0)
+            if slot is not None:
+                leave_low(slot, ed)
+            for x in range(1, 4):
+                magnetic(x)
+                electric(x)
+            electric(4)
+            if cut_to is not None:
+                cut_latest(cut_to, ed)
+            if slot is not None:
+                leave_y(slot, ed, hd)
 
         def material_window():
             each(-1, lambda m: mat_copy(m).wait_recv())
@@ -365,9 +410,10 @@
         sets = [(e2.at[q], h2.at[q], p2.at[q]) for q in range(3)]
         e_in.wait()
         h_in.wait()
-        pack_halos(0, sets[0][0], sets[0][1])
         all_here()
-        send_halos(0)
+        leave_high(0, sets[0][0], sets[0][1])
+        leave_low(0, sets[0][0])
+        leave_y(0, sets[0][0], sets[0][1])
         each(1, lambda m: pos_copy(m).start(), AROUND)
         for cp in m_in:
             cp.wait()
@@ -395,36 +441,25 @@
         ini_copy().start()
         p_in.wait()
 
-        def advance(slot, source, target):
-            put_halos(slot, source[0], target[1])
-            update(*source, *target)
+        def advance(slot_in, source, target, **then):
+            put_halos(slot_in, source[0], target[1])
+            update(*source, *target, **then)
 
         def arrive(slot):
             each(-1, lambda m: halo_copy(m, slot).wait_recv())
 
-        def leave(slot, state):
-            pack_halos(slot, state[0], state[1])
-            send_halos(slot)
-
         arrive(0)
-        advance(0, sets[0], sets[1])
-        cut_latest(0, sets[1][0])
-        leave(1, sets[1])
+        advance(0, sets[0], sets[1], slot=1, cut_to=0)
         learn_places()
         material_window()
         arrive(1)
-        advance(1, sets[1], sets[2])
-        cut_latest(1, sets[2][0])
-        leave(2, sets[2])
+        advance(1, sets[1], sets[2], slot=2, cut_to=1)
         arrive(2)
-        put_halos(2, sets[2][0], sets[0][1])
-        update(*sets[2], sets[0][0], sets[0][1], None)
-        cut_latest(2, sets[0][0])
+        advance(2, sets[2], (sets[0][0], sets[0][1], None), cut_to=2)
         del_copy(0).wait_recv()
         place(0, sets[1][0])
         mend_halos(1, 0)
-        advance(1, sets[1], sets[0])
-        leave(3, sets[0])
+        advance(1, sets[1], sets[0], slot=3)
         arrive(3)
         del_copy(1).wait_recv()
         place(1, sets[0][0])
@@ -436,9 +471,8 @@
         h_out.start()
         p_out.start()
         del_copy(STEPS - 1).wait_recv()
-        place(STEPS - 1, e)
-        e_out = pltpu.make_async_copy(e.at[:, 0:6, 0:24, :], out.at[0, 0:3], lsem.at[0])
-        e_out.start()
+        e_out = [pltpu.make_async_copy(e.at[:, x, 0:24, :], out.at[0, 0:3, x], lsem.at[12 + x]) for x in range(6)]
+        place(STEPS - 1, e, e_out)
 
         each(1, lambda m: pos_copy(m).wait_send(), AROUND)
         each(1, lambda m: mat_copy(m).wait_send())
@@ -450,7 +484,8 @@
         ini_copy().wait_send()
         h_out.wait()
         p_out.wait()
-        e_out.wait()
+        for cp in e_out:
+            cp.wait()
 
     @pl.when(jnp.logical_not(coarse))
     def _():
@@ -815,9 +850,10 @@
         return pl.pallas_call(
             functools.partial(kernel, nx, ny),
             out_shape=jax.ShapeDtypeStruct(fields.shape, F32),
-            in_specs=[pl.BlockSpec(memory_space=pl.ANY)] * 2 + [pl.BlockSpec(memory_space=pltpu.SMEM)] * 5,
+            in_specs=[pl.BlockSpec(memory_space=pl.ANY)] * 7,
             out_specs=pl.BlockSpec(memory_space=pl.ANY),
             scratch_shapes=[
+                *[pltpu.SMEM((8,), F32)] * 4, pltpu.SMEM((1, 1, 6), jnp.int32),
                 vm((3, 3, 7, 32, 384), F32), vm((3, 3, 7, 32, 384), F32), vm((3, 3, 6, 24, 384), F32), vm((5, 6, 24, 384), F32),
                 vm((3, 9, 6, 24, 128), F32), vm((3, 6, 24, 128), jnp.int32),
                 vm((9, 7, 9, 8, 128), F32), vm((5, 6, 9, 8, 128), F32),
@@ -831,7 +867,7 @@
                 vm((2, STEPS - 1, 16, 128), F32), vm((2, STEPS - 1) + region, F32), vm((8, STEPS - 1, 16, 128), F32),
                 vm((6, 3, 8, 128), jnp.int32), vm((2, 3, 24, 128), jnp.int32), vm((6, 3, 8, 128), jnp.int32),
                 vm((4, 2, 2, 8, 128), jnp.int32), vm((4, 2, 2, 8, 128), jnp.int32),
-                dma((7,)), dma((6, SETS)), dma((6, SETS)),
+                dma((18,)), dma((6, SETS)), dma((6, SETS)),
                 dma((STEPS + 1,)), dma((STEPS + 1,)), dma((STEPS,)), dma((STEPS,)),
                 dma((6, STEPS)), dma((6, STEPS)), dma((8,)), dma((8,)),
                 dma((8, STEPS)), dma((8, STEPS)), dma((6,)), dma((6,)), dma((1,)), dma((1,)),

time: 37.1 us -> 36.2 us (0.976)
  Pallas kernels: 33.9 us -> 33 us
    pallas_call x1, Pallas kernels: 33.9 us -> 33 us  [body(): pl.pallas_call(functools.partial(kernel, nx, ny), out_shape=jax.ShapeDtyp...]
where the time goes in v5:
time: 36.2 us; the launch traced here: 35.9 us
  Pallas kernels  33 us (91%)
  local copies, waits for them, and re-layouts  2.96 us (8%)
    pallas_call x1, Pallas kernels, body(): pl.pallas_call(functools.partial(kernel, nx, ny), out_shape=jax.ShapeDtyp...  33 us
    unnamed x1, local copies, waits for them, and re-layouts  2.96 us

profile of v5, /device:TPU:40, one launch (start us, length us, event | category | flops | bytes accessed | tf_op | source)
XLA Modules:
  0.0 35.9 jit_solution(9791289544528057325)
XLA Ops:
  0.0 33.0 %shard_map.73 = f32[1,9,6,24,384]{4,3,2,1,0:T(8,128)} custom-call(f32[1,9,6,24,384]{4,3,2,1,0:T(8,128)} %fields.1, s32[1,6,24,384]{3,2,1,0:T(8,128)} %material.1, f32[8]{0:T(128)} %permit_in.1, f32[8]{0:T(128)} %conduct_in.1, f32[8]{0:T(128)} %relax_in.1, f32[8]{0:T(128)} %debye_in.1, s32[1,1,6]{2,1,0:T(1,128)} %subgrids_in.1), custom_call_target="tpu_custom_call" | custom-call | tf_op jit(solution)/shard_map/pallas_call | solution.py:850
  33.0 3.0 %copy.9 = f32[1,9,6,24,384]{4,3,2,1,0:T(8,128)} copy(f32[1,9,6,24,384]{4,3,2,1,0:T(8,128)} %shard_map.73) | data formatting | bytes 3981312

commit v6 on v5

--- a/solution.py
+++ b/solution.py
@@ -223,7 +223,6 @@
         row_ok = [row_in(y0, u) for u in range(3)]
         lane_ok = [lane_in(z0, v) for v in range(3)]
         wide = lax.broadcasted_iota(jnp.int32, (24, 384), 0)
-        plane = lax.broadcasted_iota(jnp.int32, (8, 384), 0)
 
         def cut(load, i):
             tile = jnp.zeros((8, 128), F32)
@@ -289,18 +288,21 @@
         def put_halos(n, e, h):
             e[1:3, 6, 0:24, :] = xe_r[n]
             h[1, 0, 8:32, :] = flag_x * (xg_r[n, 0] + 0.5 * e[2, 0, 0:24, :])
-            corner = jnp.where(wide == 23, jnp.broadcast_to(c1_r[n, 0:1, :], (24, 384)), 0.0)
-            h[2, 0, 8:32, :] = flag_x * (xg_r[n, 1] - 0.5 * (e[1, 0, 0:24, :] - corner))
+            h[2, 0, 8:32, :] = flag_x * (xg_r[n, 1] - 0.5 * e[1, 0, 0:24, :])
             for x in range(6):
                 own[0, x:x + 1, :] = e[0, x, 0:1, :]
                 own[1, x:x + 1, :] = e[2, x, 0:1, :]
             pln[0] = flag_y * (yg_r[n, 0] - 0.5 * own[1])
-            pln[1] = flag_y * (yg_r[n, 1] + 0.5 * (own[0] - jnp.where(plane == 5, jnp.broadcast_to(c2_r[n, 0:1, :], (8, 384)), 0.0)))
+            pln[1] = flag_y * (yg_r[n, 1] + 0.5 * own[0])
             for x in range(6):
                 e[0, x, 24:25, :] = ye_r[n, 0, x:x + 1, :]
                 e[2, x, 24:25, :] = ye_r[n, 1, x:x + 1, :]
                 h[0, x + 1, 7:8, :] = pln[0, x:x + 1, :]
                 h[2, x + 1, 7:8, :] = pln[1, x:x + 1, :]
+
+        def put_corners(n, h):
+            h[2, 0, 31:32, :] = h[2, 0, 31:32, :] + (0.5 * flag_x) * c1_r[n, 0:1, :]
+            h[2, 6, 7:8, :] = h[2, 6, 7:8, :] - (0.5 * flag_y) * c2_r[n, 0:1, :]
 
         def mend_halos(n, d):
             each(-1, lambda m: near_copy(m, d).wait_recv())
@@ -335,7 +337,7 @@
                     spot = (n, slice(0, 8), slice(128 * v, 128 * v + 128))
                     ref[spot] = ref[spot] + jnp.where(lane_in(place_of[m, 2, 0], v), keep[d], 0.0)
 
-        def update(e, h, p, ed, hd, pd_, slot=None, cut_to=None):
+        def update(e, h, p, ed, hd, pd_, corners, slot=None, cut_to=None):
             def magnetic(x):
                 for u in range(3):
                     r = slice(8 * u, 8 * u + 8)
@@ -363,19 +365,17 @@
                         if pd_ is not None:
                             pd_[c, x, r, :] = kf * pol + kg * new
 
-            magnetic(4)
-            magnetic(5)
+            for x in range(6):
+                magnetic(x)
+                if 1 < x:
+                    electric(x - 1)
+            corners()
             electric(5)
             if slot is not None:
                 leave_high(slot, ed, hd)
-            magnetic(0)
             electric(0)
             if slot is not None:
                 leave_low(slot, ed)
-            for x in range(1, 4):
-                magnetic(x)
-                electric(x)
-            electric(4)
             if cut_to is not None:
                 cut_latest(cut_to, ed)
             if slot is not None:
@@ -441,30 +441,39 @@
         ini_copy().start()
         p_in.wait()
 
-        def advance(slot_in, source, target, **then):
+        def advance(slot_in, source, target, fresh, **then):
+            def corners():
+                if fresh:
+                    arrive(slot_in, (C1, C2))
+                put_corners(slot_in, target[1])
+
+            if fresh:
+                arrive(slot_in, (XE, YE, XG, YG))
             put_halos(slot_in, source[0], target[1])
-            update(*source, *target, **then)
-
-        def arrive(slot):
-            each(-1, lambda m: halo_copy(m, slot).wait_recv())
-
-        arrive(0)
-        advance(0, sets[0], sets[1], slot=1, cut_to=0)
+            update(*source, *target, corners, **then)
+
+        def arrive(slot, which):
+            for m in which:
+                dx, dy = TO_NEXT[m]
+
+                @pl.when(exists(-dx, -dy))
+                def _():
+                    halo_copy(m, slot).wait_recv()
+
+        advance(0, sets[0], sets[1], True, slot=1, cut_to=0)
         learn_places()
         material_window()
-        arrive(1)
-        advance(1, sets[1], sets[2], slot=2, cut_to=1)
-        arrive(2)
-        advance(2, sets[2], (sets[0][0], sets[0][1], None), cut_to=2)
+        advance(1, sets[1], sets[2], True, slot=2, cut_to=1)
+        advance(2, sets[2], (sets[0][0], sets[0][1], None), True, cut_to=2)
         del_copy(0).wait_recv()
         place(0, sets[1][0])
         mend_halos(1, 0)
-        advance(1, sets[1], sets[0], slot=3)
-        arrive(3)
+        advance(1, sets[1], sets[0], False, slot=3)
+        arrive(3, range(6))
         del_copy(1).wait_recv()
         place(1, sets[0][0])
         mend_halos(3, 1)
-        advance(3, sets[0], sets[2])
+        advance(3, sets[0], sets[2], False)
         e, h, p = sets[2]
         h_out = pltpu.make_async_copy(h.at[:, 1:7, 8:32, :], out.at[0, 3:6], lsem.at[1])
         p_out = pltpu.make_async_copy(p, out.at[0, 6:9], lsem.at[2])
@@ -565,7 +574,7 @@
         edge_y = {0: rows == 0, 2: rows == ly - 1}
         edge_z = {0: lanes == 0, 2: lanes == lz - 1}
 
-        def at_layer(x, carry):
+        def at_layer(x, carry, edges=True):
             ok = inside & (inside_x(x) + none > 0)
             edge = jnp.where((x == 0) | (x == 3 * lx - 1), 1, 0).astype(jnp.int32)
             edge_x = ok & (edge + none > 0)
@@ -609,19 +618,48 @@
                 for c in range(3):
                     pol = ff[6 + c, x, t]
                     new = ka * E[c, t] + kc * curls[c] + kb * pol
-                    marks = []
-                    if c != 0:
-                        marks.append(edge_x)
-                    if c != 1 and ry in ok_y:
-                        marks.append(ok_y[ry])
-                    if c != 2 and rz in ok_z:
-                        marks.append(ok_z[rz])
+                    if not edges:
+                        ff[c, x, t] = new
+                        continue
+                    marks = marked(c, ry, rz, edge_x, ok_y, ok_z)
                     if marks:
                         new = jnp.where(functools.reduce(jnp.logical_or, marks), drv[c, xc], new)
                     ff[c, x, t] = new
                     ff[6 + c, x, t] = kf * pol + new
             return carry
 
+        def marked(c, ry, rz, edge_x, ok_y, ok_z):
+            marks = []
+            if c != 0:
+                marks.append(edge_x)
+            if c != 1 and ry in ok_y:
+                marks.append(ok_y[ry])
+            if c != 2 and rz in ok_z:
+                marks.append(ok_z[rz])
+            return marks
+
+        def start_layer(x, carry):
+            return at_layer(x, carry, False)
+
+        def finish_layer(x, carry):
+            ok = inside & (inside_x(x) + none > 0)
+            edge = jnp.where((x == 0) | (x == 3 * lx - 1), 1, 0).astype(jnp.int32)
+            edge_x = ok & (edge + none > 0)
+            ok_y = {q: m & ok for q, m in edge_y.items()}
+            ok_z = {q: m & ok for q, m in edge_z.items()}
+            for ry in range(3):
+                for rz in range(3):
+                    t = 3 * ry + rz
+                    kf = fk[3, x, t]
+                    for c in range(3):
+                        new = ff[c, x, t]
+                        marks = marked(c, ry, rz, edge_x, ok_y, ok_z)
+                        if marks:
+                            new = jnp.where(functools.reduce(jnp.logical_or, marks), drv[c, x // 3], new)
+                            ff[c, x, t] = new
+                        ff[6 + c, x, t] = kf * ff[6 + c, x, t] + new
+            return carry
+
         wrows = lax.broadcasted_iota(jnp.int32, (16, 256), 0)
         wlanes = lax.broadcasted_iota(jnp.int32, (16, 256), 1)
         at_y = y0 - 4 + ((wrows - (y0 - 4)) & 15)
@@ -659,7 +697,13 @@
             for c in range(3):
                 for xr in range(-reach, 2 + reach):
                     w[c, xr] = jnp.where(region, twice(del_s[d, c, xr]), 0.0) if 0 <= xr < 2 else jnp.zeros((16, 256), F32)
-            for m, (dx, dy) in enumerate(AROUND):
+            for m in (1, 3, 0, 2, 4, 5, 6, 7):
+                dx, dy = AROUND[m]
+
+                @pl.when(exists(-dx, -dy))
+                def _():
+                    box_copy(m, d).wait_recv()
+
                 far_x, far_y, far_z = place_of[m, 0, 0], place_of[m, 1, 0], place_of[m, 2, 0]
                 ok = w_in(at_z, far_z, 128)
                 if dy == 0:
@@ -711,7 +755,6 @@
                         kw[(2,) + spot] = pick(slab[2], here) * pick(slab[4], here)
 
         def respond(n):
-            each(-1, lambda m: box_copy(m, n - 1).wait_recv(), AROUND)
             hh = {}
             if n == 1:
                 w = changes(0, 2)
@@ -749,22 +792,26 @@
                 ear[0, c, i] = to_box(ini_r[c, i])
 
         for n in range(STEPS):
+            lax.fori_loop(0, 6, start_layer, 0)
+            if n == 1:
+                window_factors()
             lat_copy(n).wait_recv()
             if n == 0:
                 for c in range(3):
                     for i in range(2):
                         ear[1, c, i] = to_box(lat_r[0, c, i])
             else:
-                if n == 1:
-                    window_factors()
                 respond(n)
+
+            drv[...] = ear[0] + (1.0 / 3.0) * (ear[1] - ear[0])
+            lax.fori_loop(0, 6, finish_layer, 0)
 
             def substep(s, carry):
                 weight = (s + 1).astype(F32) * (1.0 / 3.0)
                 drv[...] = ear[0] + weight * (ear[1] - ear[0])
                 return lax.fori_loop(0, 6, at_layer, carry, unroll=True)
 
-            lax.fori_loop(0, 3, substep, 0)
+            lax.fori_loop(1, 3, substep, 0)
             for i in range(2):
                 ok = inside & (inside_x(3 * i) + none > 0)
                 for c in range(3):
@@ -800,7 +847,12 @@
                 nd_s[0, n] = jnp.broadcast_to((high * left) * del_s[n, 0, 1, 0:1, :], (8, 128))
                 nd_s[1, n] = jnp.broadcast_to((low * right) * del_s[n, 1, 0, 7:8, :], (8, 128))
                 del_copy(n).start()
-                each(1, lambda m: near_copy(m, n).start())
+                for m in (4, 5, 0, 2, 1, 3):
+                    dx, dy = TO_NEXT[m]
+
+                    @pl.when(exists(dx, dy))
+                    def _():
+                        near_copy(m, n).start()
             else:
                 del_copy(n).start()
 

time: 36.2 us -> 35.3 us (0.975)
  Pallas kernels: 33 us -> 32.2 us
    pallas_call x1, Pallas kernels: 33 us -> 32.2 us  [body(): pl.pallas_call(functools.partial(kernel, nx, ny), out_shape=jax.ShapeDtyp...]
where the time goes in v6:
time: 35.3 us; the launch traced here: 35.2 us
  Pallas kernels  32.2 us (91%)
  local copies, waits for them, and re-layouts  2.96 us (8%)
    pallas_call x1, Pallas kernels, body(): pl.pallas_call(functools.partial(kernel, nx, ny), out_shape=jax.ShapeDtyp...  32.2 us
    unnamed x1, local copies, waits for them, and re-layouts  2.96 us

profile of v6, /device:TPU:40, one launch (start us, length us, event | category | flops | bytes accessed | tf_op | source)
XLA Modules:
  0.0 35.2 jit_solution(16435178017633678931)
XLA Ops:
  0.0 32.2 %shard_map.73 = f32[1,9,6,24,384]{4,3,2,1,0:T(8,128)} custom-call(f32[1,9,6,24,384]{4,3,2,1,0:T(8,128)} %fields.1, s32[1,6,24,384]{3,2,1,0:T(8,128)} %material.1, f32[8]{0:T(128)} %permit_in.1, f32[8]{0:T(128)} %conduct_in.1, f32[8]{0:T(128)} %relax_in.1, f32[8]{0:T(128)} %debye_in.1, s32[1,1,6]{2,1,0:T(1,128)} %subgrids_in.1), custom_call_target="tpu_custom_call" | custom-call | tf_op jit(solution)/shard_map/pallas_call | solution.py:902
  32.2 3.0 %copy.9 = f32[1,9,6,24,384]{4,3,2,1,0:T(8,128)} copy(f32[1,9,6,24,384]{4,3,2,1,0:T(8,128)} %shard_map.73) | data formatting | bytes 3981312

commit v7 on v6

--- a/solution.py
+++ b/solution.py
@@ -125,8 +125,14 @@
 
     @pl.when(coarse)
     def _():
-        for ref in (mx_r, my_r) + recvs:
+        for ref in (mx_r, my_r, c1_r, c2_r):
             ref[...] = jnp.zeros_like(ref)
+        for m in (XE, YE, XG, YG):
+            dx, dy = TO_NEXT[m]
+
+            @pl.when(jnp.logical_not(exists(-dx, -dy)))
+            def _():
+                recvs[m][...] = jnp.zeros_like(recvs[m])
 
     barrier = pltpu.get_barrier_semaphore()
     pl.semaphore_signal(barrier, inc=1, device_id=partner, device_id_type=MESH)

time: 35.3 us -> 35.3 us (level)
  no operation moved by 1% of the time
where the time goes in v7:
time: 35.3 us; the launch traced here: 35.2 us
  Pallas kernels  32.2 us (91%)
  local copies, waits for them, and re-layouts  2.96 us (8%)
    pallas_call x1, Pallas kernels, body(): pl.pallas_call(functools.partial(kernel, nx, ny), out_shape=jax.ShapeDtyp...  32.2 us
    unnamed x1, local copies, waits for them, and re-layouts  2.96 us

profile of v7, /device:TPU:40, one launch (start us, length us, event | category | flops | bytes accessed | tf_op | source)
XLA Modules:
  0.0 35.2 jit_solution(5014169705381299893)
XLA Ops:
  0.0 32.2 %shard_map.73 = f32[1,9,6,24,384]{4,3,2,1,0:T(8,128)} custom-call(f32[1,9,6,24,384]{4,3,2,1,0:T(8,128)} %fields.1, s32[1,6,24,384]{3,2,1,0:T(8,128)} %material.1, f32[8]{0:T(128)} %permit_in.1, f32[8]{0:T(128)} %conduct_in.1, f32[8]{0:T(128)} %relax_in.1, f32[8]{0:T(128)} %debye_in.1, s32[1,1,6]{2,1,0:T(1,128)} %subgrids_in.1), custom_call_target="tpu_custom_call" | custom-call | tf_op jit(solution)/shard_map/pallas_call | solution.py:908
  32.2 3.0 %copy.9 = f32[1,9,6,24,384]{4,3,2,1,0:T(8,128)} copy(f32[1,9,6,24,384]{4,3,2,1,0:T(8,128)} %shard_map.73) | data formatting | bytes 3981312
